TPU v7x, 32 devices: a whole 2x2x4 slice. The times are simulated.
32 devices in a mesh: groups: 2 (over y), tiles: 4 (over z), band: 2 (over x), rep: 2 (over core).
Axes of the slice: x: 2, y: 2, z: 4, core: 2. Of those that a mesh axis runs over, the one named last changes fastest.
Arguments:
- features: bfloat16 [8, 16, 2, 16, 128], P(('groups', 'band'), 'tiles'), parts along dimension 0, may hold values from -6 to 6
- state: float32 [8, 16, 16, 16, 128], P(('groups', 'band'), 'tiles'), parts along dimension 0, may hold values from -3 to 3
- live: int32 [16], P('tiles'), may hold values from 0 to 1, as said below
- neighbours: int32 [16, 2], P('tiles'), may hold values from -1 to 15, as said below
- coarse_perm: int32 [4, 4], P('tiles'), may hold values from 0 to 3, as said below
- coarse_state: float32 [32, 16, 4, 32], P(('groups', 'tiles', 'band')), parts along dimension 0, may hold values from -3 to 3
- w_update: bfloat16 [9, 16, 18], replicated, may hold values from -0.5 to 0.5
- b_update: float32 [16], replicated, may hold values from -3 to 3
- w_reset: bfloat16 [9, 16, 18], replicated, may hold values from -0.5 to 0.5
- b_reset: float32 [16], replicated, may hold values from -3 to 3
- w_cand: bfloat16 [9, 16, 18], replicated, may hold values from -0.5 to 0.5
- b_cand: float32 [16], replicated, may hold values from -3 to 3
- u_pool: float32 [16, 16], replicated, may hold values from -1.5 to 1.5
- u_state: float32 [16, 16], replicated, may hold values from -1.5 to 1.5
- b_coarse: float32 [16], replicated, may hold values from -3 to 3
Outputs:
- new_state: float32 [8, 16, 16, 16, 128], P(('groups', 'band'), 'tiles', 'rep'), parts along dimension 0
- coarse_next: float32 [32, 16, 4, 32], P(('groups', 'tiles', 'band')), parts along dimension 0
There are 2 independent parts, one for each index of `groups`. A program takes and returns all parts, laid end to end along the dimension named above; an argument that names none is the same for every part. Nothing has to cross between parts.
Inputs may be any that keep to these rules, and one draw needn't show every extreme that they name: Every device of tiles has between 1 and 4 live slots, at any positions; in every draw some device has all 4 live. `neighbours`: the live tiles form one vertical chain that passes the devices of tiles in index order, each device's live tiles forming one run of the chain in some order; entry 0 names the tile above, entry 1 the tile below, -1 at the chain's two ends and in both entries of an empty slot. `coarse_perm`: each row is a permutation of 0 to 3.
All inputs are finite; a program needn't handle non-finite values.
Results may differ from a plain program's by a relative error of at most 0.0013.
Values may be sent and summed in bfloat16 or wider, within the bound.
A program may use at most 64 MiB of HBM per device.

v0:
```python
import jax
import jax.numpy as jnp
from jax import lax
from jax.sharding import PartitionSpec as P


def padded(block, sides, width):
    for axis, dim in sides:
        count = lax.axis_size(axis)
        forward = [(i, i + 1) for i in range(count - 1)]
        backward = [(target, source) for source, target in forward]
        low = lax.ppermute(
            lax.slice_in_dim(block, block.shape[dim] - width, None, axis=dim), axis, forward
        )
        high = lax.ppermute(lax.slice_in_dim(block, 0, width, axis=dim), axis, backward)
        block = jnp.concatenate([low, block, high], axis=dim)
    return block


def apply_filter(
    padded_input, filter_weight, dilation_rate, first_row_index, row_count, column_count
):
    total = None
    for left_operand in (-1, 0, 1):
        for right_operand in (-1, 0, 1):
            window_slice = padded_input[
                :,
                :,
                :,
                first_row_index
                + left_operand * dilation_rate : first_row_index
                + left_operand * dilation_rate
                + row_count,
                2
                + right_operand * dilation_rate : 2
                + right_operand * dilation_rate
                + column_count,
            ]
            term = jnp.einsum(
                "oi,bsirw->bsorw",
                filter_weight[(left_operand + 1) * 3 + (right_operand + 1)],
                window_slice,
                preferred_element_type=jnp.float32,
            )
            total = term if total is None else total + term
    return total


def choose_rows(block, select):
    masked = jnp.where(select[None, :, None, None, None], block, jnp.zeros_like(block))
    return jnp.sum(masked, axis=1)


def shards(
    features,
    state,
    live,
    neighbours,
    coarse_perm,
    coarse_state,
    w_update,
    b_update,
    w_reset,
    b_reset,
    w_cand,
    b_cand,
    u_pool,
    u_state,
    b_coarse,
):
    slots = state.shape[1]
    chans = state.shape[2]
    row_count = state.shape[3]
    column_count = state.shape[4]
    inputs_count = features.shape[2]
    half = chans // lax.axis_size("rep")
    start = lax.axis_index("rep") * half
    base = lax.axis_index("tiles") * slots
    ups = neighbours[:, 0]
    downs = neighbours[:, 1]
    up_here = (ups >= base) & (ups < base + slots)
    down_here = (downs >= base) & (downs < base + slots)
    up_far = (ups >= 0) & jnp.logical_not(up_here)
    down_far = (downs >= 0) & jnp.logical_not(down_here)
    alive = live > 0
    first_sel = alive & jnp.logical_not(up_here)
    last_sel = alive & jnp.logical_not(down_here)

    def own_out(filter_weight):
        return lax.dynamic_slice_in_dim(filter_weight, start, half, 1)

    def own_bias(bias):
        return lax.dynamic_slice_in_dim(bias, start, half, 0)[:, None, None]

    hb = state.astype(jnp.bfloat16)
    joined = jnp.concatenate([features, hb], axis=2)
    top = choose_rows(joined[:, :, :, :3, :], first_sel)
    bottom = choose_rows(joined[:, :, :, row_count - 3 :, :], last_sel)
    cycle = padded(jnp.concatenate([top, bottom], axis=2), (("tiles", 2),), 3)
    cycle_prev = cycle[:, None, :, :3, :]
    cycle_next = cycle[:, None, :, 3 * 3 : 4 * 3, :]
    top_local = jnp.take(
        joined[:, :, :, row_count - 3 :, :], jnp.clip(ups - base, 0, slots - 1), axis=1
    )
    bottom_local = jnp.take(joined[:, :, :, :3, :], jnp.clip(downs - base, 0, slots - 1), axis=1)
    zeros_rows = jnp.zeros_like(top_local)
    top = jnp.where(
        up_here[None, :, None, None, None],
        top_local,
        jnp.where(up_far[None, :, None, None, None], cycle_prev + zeros_rows, zeros_rows),
    )
    bottom = jnp.where(
        down_here[None, :, None, None, None],
        bottom_local,
        jnp.where(down_far[None, :, None, None, None], cycle_next + zeros_rows, zeros_rows),
    )
    full = jnp.concatenate([top, joined, bottom], axis=3)
    first = jnp.pad(full, ((0, 0), (0, 0), (0, 0), (0, 0), (2, 2)))
    update = jax.nn.sigmoid(
        apply_filter(first, own_out(w_update), 1, 3, row_count, column_count) + own_bias(b_update)
    )
    hidden_wide = first[:, :, inputs_count:, 1 : row_count + 5, 2 : column_count + 2]
    reset_half = jax.nn.sigmoid(
        apply_filter(first, own_out(w_reset), 1, 1, row_count + 4, column_count) + own_bias(b_reset)
    )
    wide_half = lax.dynamic_slice_in_dim(hidden_wide, start, half, 2)
    gated = lax.all_gather(
        (reset_half * wide_half.astype(jnp.float32)).astype(jnp.bfloat16), "rep", axis=2, tiled=True
    )
    gated_pad = jnp.pad(gated, ((0, 0), (0, 0), (0, 0), (0, 0), (2, 2)))
    second = jnp.concatenate([first[:, :, :inputs_count, 1 : row_count + 5, :], gated_pad], axis=2)
    candidate = jnp.tanh(
        apply_filter(second, own_out(w_cand), 2, 2, row_count, column_count) + own_bias(b_cand)
    )
    state_half = lax.dynamic_slice_in_dim(state, start, half, 2)
    live_scale = alive.astype(jnp.float32)[None, :, None, None, None]
    new_half = ((1.0 - update) * state_half + update * candidate) * live_scale
    band_local = new_half.shape[0]
    blocks = new_half.reshape(band_local, slots, half, row_count // 4, 4, column_count // 4, 4)
    pooled = jnp.sum(jnp.sum(blocks, axis=(4, 6)), axis=0) / 16.0
    ordered = jnp.take(pooled, coarse_perm[0], axis=0)
    owned = lax.psum_scatter(ordered, "band", scatter_dimension=0, tiled=True)
    pooled_all = lax.all_gather(owned, "rep", axis=1, tiled=True)
    pre = jnp.einsum("oc,kcij->koij", u_pool, pooled_all, precision=lax.Precision.HIGHEST)
    pre = pre + jnp.einsum("oc,kcij->koij", u_state, coarse_state, precision=lax.Precision.HIGHEST)
    pre = pre + b_coarse[None, :, None, None]
    coarse_next = coarse_state + jnp.tanh(pre)
    return (new_half, coarse_next)


def solution(mesh):
    return jax.shard_map(
        shards,
        mesh=mesh,
        in_specs=(
            P(("groups", "band"), "tiles", None, None, None),
            P(("groups", "band"), "tiles", None, None, None),
            P("tiles"),
            P("tiles", None),
            P("tiles", None),
            P(("groups", "tiles", "band"), None, None, None),
            P(),
            P(),
            P(),
            P(),
            P(),
            P(),
            P(),
            P(),
            P(),
        ),
        out_specs=(
            P(("groups", "band"), "tiles", "rep", None, None),
            P(("groups", "tiles", "band"), None, None, None),
        ),
        check_vma=False,
    )
```

profile of v0, /device:TPU:0, one launch (start us, length us, event | category | flops | bytes accessed | tf_op | source)
XLA Modules:
  0.0 65.9 jit_solution(5684396351804242542)
XLA Ops:
  7.3 0.8 %not_and_fusion = (pred[4]{0:T(512)(128)(4,1)S(1)}, pred[4]{0:T(512)(128)(4,1)S(1)}) fusion(s32[4]{0:T(128)} %param.19, s32[]{:T(128)S(6)} %add.187, s32[]{:T(128)S(6)} %mul.23, s32[4,2]{0,1:T(2,128)} %param.20), kind=kLoop, calls=%fused_computation.176 | loop fusion | flops 24 | bytes 48 | tf_op jit(solution)/shard_map/and | solution.py:87
  8.0 0.8 %compare_and_fusion.1 = (pred[4]{0:T(512)(128)(4,1)S(1)}, s32[4]{0:T(128)S(1)}, pred[4]{0:T(512)(128)(4,1)S(1)}, pred[4]{0:T(512)(128)(4,1)S(1)}, s32[4]{0:T(128...) fusion(s32[]{:T(128)S(6)} %mul.23, s32[4,2]{0,1:T(2,128)} %param.20, ...), kind=kLoop, calls=%fused_computation.172 | loop fusion | flops 124 | bytes 116 | tf_op jit(solution)/shard_map/jit(_take)/and | solution.py:102
  8.8 0.7 %fusion.109 = (f32[4]{0:T(128)S(1)}, pred[4]{0:T(512)(128)(4,1)S(1)}) fusion(s32[4]{0:T(128)} %param.19, pred[4]{0:T(512)(128)(4,1)S(1)} %get-tuple-element.27), kind=kLoop, calls=%fused_computation.180 | loop fusion | flops 16 | bytes 40 | tf_op jit(solution)/shard_map/convert_element_type | solution.py:136
  9.5 1.6 %copy.83 = bf16[2,4,16,16,128]{4,2,3,1,0:T(8,128)(2,1)S(1)} copy(f32[2,4,16,16,128]{4,3,2,1,0:T(8,128)} %param.18) | data formatting | bytes 1572864 | tf_op args[1]
  11.1 0.9 %copy.36 = bf16[2,4,2,16,128]{4,2,3,1,0:T(2,128)(2,1)S(1)} copy(bf16[2,4,2,16,128]{4,3,2,1,0:T(8,128)(2,1)} %param.17) | data formatting | bytes 131072 | tf_op args[0]
  12.2 1.3 %collective-permute-start.1 = (bf16[2,18,3,128]{3,1,2,0:T(8,128)(2,1)S(1)}, bf16[2,18,3,128]{3,1,2,0:T(8,128)(2,1)S(1)}, u32[]{:S(2)}, u32[]{:S(2)}) collective-permute-start(bf16[2,18,3,128]{3,1,2,0:T(8,128)(2,1)S(1)} %get-tuple-element.21), channel_id=1, source_target_pairs={{4,0},{8,4},{12,8},{5,1},{9,5},{13,9},{6,2},{10,6},{14,10},{7,3},{... | collective-permute-start | bytes 82952 | tf_op jit(solution)/shard_map/ppermute | solution.py:15
  13.5 5.6 %collective-permute-start = (bf16[2,18,3,128]{3,1,2,0:T(8,128)(2,1)S(1)}, bf16[2,18,3,128]{3,1,2,0:T(8,128)(2,1)S(1)}, u32[]{:S(2)}, u32[]{:S(2)}) collective-permute-start(bf16[2,18,3,128]{3,1,2,0:T(8,128)(2,1)S(1)} %get-tuple-element.9), channel_id=1, source_target_pairs={{0,4},{4,8},{8,12},{1,5},{5,9},{9,13},{2,6},{6,10},{10,14},{3,7},{... | collective-permute-start | bytes 82952 | tf_op jit(solution)/shard_map/ppermute | solution.py:12
  19.8 0.6 gather_fusion.2
  20.4 0.8 %gather_fusion.1 = bf16[4,2,18,3,128]{4,1,3,2,0:T(2,128)(2,1)S(1)} fusion(bf16[2,4,18,3,128]{4,0,3,2,1:T(2,128)(2,1)S(1)} %copy.37, s32[1024]{0:T(1024)S(1)} %pad_clamp_fusion.2), kind=kCustom, calls=%fused_computation.clone | custom fusion | bytes 221200 | tf_op jit(solution)/shard_map/jit(_take)/gather | solution.py:102
  23.4 0.4 convolution_add_fusion.5
  24.2 0.4 convolution_add_fusion.4
  25.0 0.4 convolution_add_fusion.3
  26.5 0.4 convolution_add_fusion.2
  27.4 0.4 convolution_add_fusion.1
  28.5 0.5 fusion.20
  29.0 2.5 %all_gather.6 = bf16[2,4,16,20,128]{4,2,3,1,0:T(8,128)(2,1)S(1)} all-gather(bf16[2,4,8,20,128]{4,2,3,1,0:T(8,128)(2,1)S(1)} %fusion.20), channel_id=1, replica_groups=mesh['groups'=2,'tiles'=4,'band'=2,'rep'=2] {'rep'}, dimensions={2}, use_global_device_ids=true | all-gather | bytes 983040 | tf_op jit(solution)/shard_map/all_gather | solution.py:127
  31.5 1.1 %fusion.1 = bf16[2,4,18,20,132]{4,2,3,1,0:T(8,128)(2,1)S(1)} fusion(bf16[2,4,16,20,128]{4,2,3,1,0:T(8,128)(2,1)S(1)} %all_gather.6, bf16[2,4,2,20,132]{4,2,3,1,0:T(2,128)(2,1)S(1)} %pad_slice_fusion.6), kind=kLoop, calls=%fused_computation.18 | loop fusion | flops 2280960 | bytes 1500160 | tf_op jit(solution)/shard_map/concatenate | solution.py:131
  32.9 0.4 convolution_add_fusion.17
  33.3 0.4 convolution_add_fusion.16
  33.9 0.4 convolution_add_fusion.14
  34.3 0.4 convolution_add_fusion.13
  35.0 0.4 convolution_add_fusion.11
  35.4 0.4 fusion.13
  35.8 0.4 fusion.125
  36.3 2.6 %copy.41 = f32[4,8,16,128]{1,3,2,0:T(8,128)} copy(f32[4,8,16,128]{3,1,2,0:T(8,128)S(1)} %get-tuple-element.30) | data formatting | bytes 524288 | tf_op jit(solution)/shard_map/reduce_sum | solution.py:140
  38.9 3.6 %reduce_sum.48 = f32[4,8,4,32]{1,3,2,0:T(8,128)S(1)} reduce(f32[4,8,4,4,32,4]{1,5,4,3,2,0:T(4,128)} %bitcast.250, f32[]{:T(128)} %constant.53.clone.1), dimensions={3,5}, to_apply=%region_3.5 | reduce | flops 61440 | bytes 278532 | tf_op jit(solution)/shard_map/reduce_sum | solution.py:140
  42.6 0.6 gather_fusion
  43.2 0.7 %broadcast_select_fusion = f32[4,8,4,32]{3,1,2,0:T(8,128)} fusion(f32[4,8,4,32]{3,1,2,0:T(8,128)S(1)} %gather_fusion, pred[4]{0:T(512)(128)(4,1)S(1)} %get-tuple-element.32), kind=kLoop, calls=%fused_computation.102 | loop fusion | flops 4096 | bytes 32772 | tf_op jit(solution)/shard_map/jit(_take)/select_n | solution.py:141
  43.9 0.9 %copy.45 = f32[2,4,8,16,128]{4,3,2,1,0:T(8,128)} copy(f32[2,4,8,16,128]{4,2,3,1,0:T(8,128)S(1)} %get-tuple-element.31) | data formatting | bytes 1048576
  44.8 10.9 %reduce-scatter.2.cloned.1.call-done = f32[2,8,4,32]{3,1,2,0:T(8,128)} async-done(((f32[4,8,4,32]{3,1,2,0:T(8,128)}), f32[2,8,4,32]{3,1,2,0:T(8,128)}) %reduce-scatter.2.cloned.1.call-update) | async-done | bytes 8208 | tf_op jit(solution)/shard_map/reduce_scatter | solution.py:142
  55.7 2.3 %all_gather.7 = f32[2,16,4,32]{3,1,2,0:T(8,128)S(1)} all-gather(f32[2,8,4,32]{3,1,2,0:T(8,128)} %reduce-scatter.2.cloned.1.call-done), channel_id=1, replica_groups=mesh['groups'=2,'tiles'=4,'band'=2,'rep'=2] {'rep'}, dimensions={1}, use_global_device_ids=true | all-gather | bytes 24576 | tf_op jit(solution)/shard_map/all_gather | solution.py:143
  58.4 0.7 copy.46
  (61 shorter events, 7.2 us)
Async XLA Ops:
  7.2 15.9 %copy-start = (bf16[9,16,18]{2,1,0:T(8,128)(2,1)S(1)}, bf16[9,16,18]{2,1,0:T(8,128)(2,1)}, u32[]{:S(2)}) copy-start(bf16[9,16,18]{2,1,0:T(8,128)(2,1)} %param.25) | copy-start | bytes 15556
  7.2 11.9 %copy-start.8 = (s32[1,4]{1,0:T(1,128)S(1)}, s32[1,4]{1,0:T(1,128)}, u32[]{:S(2)}) copy-start(s32[1,4]{1,0:T(1,128)} %param.21) | copy-start | bytes 52
  7.2 11.9 %copy-start.1 = (f32[2,4,16,16,128]{4,3,2,1,0:T(8,128)S(1)}, f32[2,4,16,16,128]{4,3,2,1,0:T(8,128)}, u32[]{:S(2)}) copy-start(f32[2,4,16,16,128]{4,3,2,1,0:T(8,128)} %param.18) | copy-start | bytes 3145732
  7.2 48.5 %reduce-scatter.2.cloned.1.call-start = ((), (), s32[]{:S(2)}) async-start(), calls=%async_computation.1 | async-start | bytes 98304 | tf_op jit(solution)/shard_map/reduce_scatter | solution.py:142
  11.0 8.5 %copy-start.9 = (f32[16]{0:T(128)S(1)}, f32[16]{0:T(128)}, u32[]{:S(2)}) copy-start(f32[16]{0:T(128)} %param.24) | copy-start | bytes 196
  11.1 8.6 %copy-start.10 = (f32[16]{0:T(128)S(1)}, f32[16]{0:T(128)}, u32[]{:S(2)}) copy-start(f32[16]{0:T(128)} %param.28) | copy-start | bytes 196
  11.1 8.6 %copy-start.11 = (f32[16]{0:T(128)S(1)}, f32[16]{0:T(128)}, u32[]{:S(2)}) copy-start(f32[16]{0:T(128)} %param.26) | copy-start | bytes 196
  12.2 9.0 %collective-permute-start.1 = (bf16[2,18,3,128]{3,1,2,0:T(8,128)(2,1)S(1)}, bf16[2,18,3,128]{3,1,2,0:T(8,128)(2,1)S(1)}, u32[]{:S(2)}, u32[]{:S(2)}) collective-permute-start(bf16[2,18,3,128]{3,1,2,0:T(8,128)(2,1)S(1)} %get-tuple-element.21), channel_id=1, source_target_pairs={{4,0},{8,4},{12,8},{5,1},{9,5},{13,9},{6,2},{10,6},{14,10},{7,3},{... | collective-permute-start | bytes 82952 | tf_op jit(solution)/shard_map/ppermute | solution.py:15
  13.5 7.8 %collective-permute-start = (bf16[2,18,3,128]{3,1,2,0:T(8,128)(2,1)S(1)}, bf16[2,18,3,128]{3,1,2,0:T(8,128)(2,1)S(1)}, u32[]{:S(2)}, u32[]{:S(2)}) collective-permute-start(bf16[2,18,3,128]{3,1,2,0:T(8,128)(2,1)S(1)} %get-tuple-element.9), channel_id=1, source_target_pairs={{0,4},{4,8},{8,12},{1,5},{5,9},{9,13},{2,6},{6,10},{10,14},{3,7},{... | collective-permute-start | bytes 82952 | tf_op jit(solution)/shard_map/ppermute | solution.py:12
  21.4 0.9 %copy-start.6 = (bf16[9,16,18]{2,1,0:T(8,128)(2,1)S(1)}, bf16[9,16,18]{2,1,0:T(8,128)(2,1)}, u32[]{:S(2)}) copy-start(bf16[9,16,18]{2,1,0:T(8,128)(2,1)} %param.23) | copy-start | bytes 15556
  29.0 3.6 %copy-start.3 = (bf16[9,16,18]{2,1,0:T(8,128)(2,1)S(1)}, bf16[9,16,18]{2,1,0:T(8,128)(2,1)}, u32[]{:S(2)}) copy-start(bf16[9,16,18]{2,1,0:T(8,128)(2,1)} %param.27) | copy-start | bytes 15556
  38.9 19.1 %copy-start.4 = (f32[16,16]{1,0:T(8,128)S(1)}, f32[16,16]{1,0:T(8,128)}, u32[]{:S(2)}) copy-start(f32[16,16]{1,0:T(8,128)} %param.29) | copy-start | bytes 3076
  42.4 15.7 %copy-start.2 = (f32[2,16,4,32]{3,2,1,0:T(4,128)S(1)}, f32[2,16,4,32]{3,2,1,0:T(4,128)}, u32[]{:S(2)}) copy-start(f32[2,16,4,32]{3,2,1,0:T(4,128)} %param.22) | copy-start | bytes 49156
  42.5 15.7 %copy-start.5 = (f32[16,16]{1,0:T(8,128)S(1)}, f32[16,16]{1,0:T(8,128)}, u32[]{:S(2)}) copy-start(f32[16,16]{1,0:T(8,128)} %param.30) | copy-start | bytes 3076
  42.5 15.7 %copy-start.7 = (f32[16]{0:T(128)S(1)}, f32[16]{0:T(128)}, u32[]{:S(2)}) copy-start(f32[16]{0:T(128)} %param.31) | copy-start | bytes 196
Sparse Core Ops, SparseCore 0:
  44.0 11.6 reduce-scatter.1
where the time goes:
time: 66.3 us; the launch traced here: 65.9 us
  between operations  14.4 us (22%)
  waiting for transfers between devices  10.9 us (16%)
  matrix products  10.7 us (16%)
  local copies, waits for them, and re-layouts  9.87 us (15%)
  other arithmetic  8.41 us (13%)
  starting transfers between devices  6.89 us (10%)
  blocking collectives  4.73 us (7%)
    reduce_scatter x1, waiting for transfers between devices, shards(): owned = lax.psum_scatter(ordered, 'band', scatter_dimension=0, tiled=True)  10.9 us
    dot_general x27, matrix products, apply_filter(): jnp.einsum('oi,bsirw->bsorw', filter_weight[(left_operand + 1) * 3 + (rig...  10.3 us
    ppermute x1, starting transfers between devices, padded(): lax.ppermute(lax.slice_in_dim(block, block.shape[dim] - width, None, axis...  5.56 us
    unnamed x29, local copies, waits for them, and re-layouts  4.41 us
    reduce_sum x1, other arithmetic, shards(): pooled = jnp.sum(jnp.sum(blocks, axis=(4, 6)), axis=0) / 16.0  3.57 us
    reduce_sum x2, local copies, waits for them, and re-layouts, shards(): pooled = jnp.sum(jnp.sum(blocks, axis=(4, 6)), axis=0) / 16.0  2.71 us
    all_gather x1, blocking collectives, shards(): lax.all_gather((reset_half * wide_half.astype(jnp.float32)).astype(jnp.bf...  2.46 us
    all_gather x1, blocking collectives, shards(): pooled_all = lax.all_gather(owned, 'rep', axis=1, tiled=True)  2.27 us
  transfers between devices with their start and end apart: 3, of which 1 were waited for; matrix products, arithmetic and copies ran while one was open for 5% of the time, Pallas kernels for 0%

commit v1 on v0

v1 whole, which is shorter than its diff:
```python
import functools

import jax
import jax.numpy as jnp
from jax import lax
from jax.experimental import pallas as pl
from jax.experimental.pallas import tpu as pltpu
from jax.sharding import PartitionSpec as P

MESH = pl.DeviceIdType.MESH
HIGHEST = lax.Precision.HIGHEST
F32 = jnp.float32
BF16 = jnp.bfloat16


def iota(shape, dim):
    return lax.broadcasted_iota(jnp.int32, shape, dim)


def sigmoid(x):
    return 0.5 * jnp.tanh(0.5 * x) + 0.5


def shifted(x, step):
    width = x.shape[1]
    wide = pltpu.roll(x.astype(F32), (-step) % width, 1)
    column = iota(x.shape, 1) + step
    return jnp.where((column >= 0) & (column < width), wide, 0.0).astype(BF16)


def kernel(
    nt, nb, nr,
    features, state, live, nbrs, perm, cs, wu, bu, wr, br, wc, bc, u_pool, u_state, b_coarse,
    out, cout,
    mains, tops, bots, send_up, send_dn, wexp, t1, t2, x1, x2, parts, csl,
    up_sems, dn_sems, pool_send, pool_recv,
):
    bands, slots, chans, rows, cols = state.shape
    ins = features.shape[2]
    half = chans // nr
    width = ins + chans
    own, cw = cs.shape[0], cs.shape[3]
    km, kh = width * rows, width * 8
    ks = km + 2 * kh
    kt = 3 * ks
    tile = lax.axis_index("tiles")
    band = lax.axis_index("band")
    rep = lax.axis_index("rep")
    base = tile * slots
    npeer = nb * nr
    me = band * nr + rep
    start = rep * half

    barrier = pltpu.get_barrier_semaphore()

    @pl.when(tile > 0)
    def _():
        pl.semaphore_signal(barrier, inc=1, device_id={"tiles": tile - 1}, device_id_type=MESH)

    @pl.when(tile < nt - 1)
    def _():
        pl.semaphore_signal(barrier, inc=1, device_id={"tiles": tile + 1}, device_id_type=MESH)

    for d in range(1, npeer):
        peer = lax.rem(me + d, npeer)
        pl.semaphore_signal(
            barrier, inc=1, device_id={"band": peer // nr, "rep": lax.rem(peer, nr)}, device_id_type=MESH
        )

    first = jnp.int32(0)
    last = jnp.int32(0)
    for s in range(slots):
        u, d = nbrs[s, 0], nbrs[s, 1]
        alive = live[s] > 0
        first = jnp.where(alive & ((u < base) | (u >= base + slots)), s, first)
        last = jnp.where(alive & ((d < base) | (d >= base + slots)), s, last)
    for b in range(bands):
        f, h = features[b, first].astype(F32)[:, :8], state[b, first, :, :8]
        send_up[b] = jnp.concatenate([f, h], axis=0).reshape(kh, cols).astype(BF16)
        f, h = features[b, last].astype(F32)[:, rows - 8 :], state[b, last, :, rows - 8 :]
        send_dn[b] = jnp.concatenate([f, h], axis=0).reshape(kh, cols).astype(BF16)

    has_up, has_dn = tile > 0, tile < nt - 1
    pl.semaphore_wait(barrier, npeer - 1 + jnp.where(has_up, 1, 0) + jnp.where(has_dn, 1, 0))

    def copy_up():
        return pltpu.make_async_remote_copy(
            send_up, tops.at[slots], up_sems.at[0], up_sems.at[1],
            device_id={"tiles": tile - 1}, device_id_type=MESH,
        )

    def copy_dn():
        return pltpu.make_async_remote_copy(
            send_dn, bots.at[slots], dn_sems.at[0], dn_sems.at[1],
            device_id={"tiles": tile + 1}, device_id_type=MESH,
        )

    @pl.when(has_up)
    def _():
        copy_up().start()

    @pl.when(has_dn)
    def _():
        copy_dn().start()

    @pl.when(jnp.logical_not(has_up))
    def _():
        bots[slots] = jnp.zeros((bands, kh, cols), BF16)

    @pl.when(jnp.logical_not(has_dn))
    def _():
        tops[slots] = jnp.zeros((bands, kh, cols), BF16)

    for s in range(slots):
        for b in range(bands):
            f = features[b, s].astype(F32)
            h = state[b, s]
            j = jnp.concatenate([f, h], axis=0)
            mains[s, b] = j.reshape(km, cols).astype(BF16)
            tops[s, b] = j[:, :8].reshape(kh, cols).astype(BF16)
            bots[s, b] = j[:, rows - 8 :].reshape(kh, cols).astype(BF16)
    tops[slots + 1] = jnp.zeros((bands, kh, cols), BF16)
    bots[slots + 1] = jnp.zeros((bands, kh, cols), BF16)

    def lanes(shape):
        k = iota(shape, len(shape) - 1)
        side = (k >= ks).astype(jnp.int32) + (k >= 2 * ks).astype(jnp.int32)
        q = k - ks * side
        up, dn = q >= km, q >= km + kh
        hq = jnp.where(dn, q - (km + kh), q - km)
        chan = jnp.where(up, hq >> 3, q >> 4)
        row = jnp.where(up, (hq & 7) + jnp.where(dn, rows, -8), q & (rows - 1))
        return side, chan, row

    side, chan, _ = lanes((width, kt))
    spread = jnp.zeros((9 * chans, kt), F32)
    for b in range(3):
        stack = jnp.concatenate([w[3 * a + b] for w in (wu, wr, wc) for a in range(3)], axis=0)
        pick = ((side == b) & (chan == iota((width, kt), 0))).astype(F32).astype(BF16)
        spread = spread + jnp.dot(stack, pick, preferred_element_type=F32)
    wexp[...] = spread.reshape(9, chans, kt)

    def fill(target, at, gate, outs, count, first_row, dilation):
        _, _, row = lanes((count, kt))
        delta = row - (iota((count, kt), 0) + first_row)
        hits = [delta == a * dilation for a in (-1, 0, 1)]

        def step(o, carry):
            total = jnp.zeros((count, kt), F32)
            for a in range(3):
                total = jnp.where(hits[a], wexp[3 * gate + a, pl.ds(outs + o, 1), :], total)
            target[pl.ds(pl.multiple_of(at + o * count, count), count), :] = total.astype(BF16)
            return carry

        return step

    def fill_halo(at, first_row):
        _, _, row = lanes((16, kt))
        which = iota((16, kt), 0)
        delta = row - ((which & 7) + first_row)
        hits = [delta == a for a in (-1, 0, 1)]

        def step(o, carry):
            total = jnp.zeros((16, kt), F32)
            for a in range(3):
                lo = wexp[3 + a, pl.ds(2 * o, 1), :]
                hi = wexp[3 + a, pl.ds(2 * o + 1, 1), :]
                total = jnp.where(hits[a], jnp.where(which < 8, lo, hi), total)
            t1[pl.ds(pl.multiple_of(at + o * 16, 16), 16), :] = total.astype(BF16)
            return carry

        return step

    mu = half * rows
    lax.fori_loop(0, half, fill(t1, 0, 0, start, rows, 0, 1), 0)
    lax.fori_loop(0, chans, fill(t1, mu, 1, 0, rows, 0, 1), 0)
    lax.fori_loop(0, chans // 2, fill_halo(mu + chans * rows, -8), 0)
    lax.fori_loop(0, chans // 2, fill_halo(mu + chans * rows + chans * 8, rows), 0)
    lax.fori_loop(0, half, fill(t2, 0, 2, start, rows, 0, 2), 0)

    csl[...] = jnp.zeros_like(csl)
    for k in range(own):
        for i in range(cs.shape[2]):
            csl[:, i * cols + k * cw : i * cols + (k + 1) * cw] = cs[k, :, i, :]
    coarse_bias = jnp.zeros((chans, 1), F32)
    for o in range(chans):
        coarse_bias = jnp.where(iota((chans, 1), 0) == o, b_coarse[o], coarse_bias)

    @pl.when(has_up)
    def _():
        copy_up().wait_send()

    @pl.when(has_dn)
    def _():
        copy_up().wait_recv()

    @pl.when(has_dn)
    def _():
        copy_dn().wait_send()

    @pl.when(has_up)
    def _():
        copy_dn().wait_recv()

    def place(s, side):
        n = nbrs[s, side]
        here = (n >= base) & (n < base + slots)
        return jnp.where(here, n - base, jnp.where(n >= 0, slots, slots + 1))

    def one_slot(s, pooled):
        above, below = place(s, 0), place(s, 1)
        pieces = []
        for b in range(bands):
            main, up, dn = mains[s, b], bots[above, b], tops[below, b]
            pieces.append((main, up, dn))
            x = jnp.concatenate([main, up, dn], axis=0)
            at = slice(b * cols, (b + 1) * cols)
            x1[0:ks, at] = shifted(x, -1)
            x1[ks : 2 * ks, at] = x
            x1[2 * ks :, at] = shifted(x, 1)
        acc = jnp.dot(t1[...], x1[...], preferred_element_type=F32)
        fm, fh = ins * rows, ins * 8
        for b in range(bands):
            at = slice(b * cols, (b + 1) * cols)
            main, up, dn = pieces[b]
            parts2 = []
            row = mu
            for piece, skip, count in ((main, fm, rows), (up, fh, 8), (dn, fh, 8)):
                held = piece.astype(F32)
                parts2.append(held[:skip])
                for o in range(chans):
                    reset = sigmoid(acc[row : row + count, at] + br[o])
                    parts2.append(reset * held[skip + o * count : skip + (o + 1) * count])
                    row += count
            x = jnp.concatenate(parts2, axis=0).astype(BF16)
            x2[0:ks, at] = shifted(x, -2)
            x2[ks : 2 * ks, at] = x
            x2[2 * ks :, at] = shifted(x, 2)
        acc2 = jnp.dot(t2[...], x2[...], preferred_element_type=F32)
        scale = live[s].astype(F32)
        summed = []
        for o in range(half):
            both = None
            for b in range(bands):
                at = slice(b * cols, (b + 1) * cols)
                update = sigmoid(acc[o * rows : (o + 1) * rows, at] + bu[start + o])
                cand = jnp.tanh(acc2[o * rows : (o + 1) * rows, at] + bc[start + o])
                new = ((1.0 - update) * state[b, s, start + o] + update * cand) * scale
                out[b, s, o] = new
                both = new if both is None else both + new
            summed.append(both)
        summed = jnp.concatenate(summed, axis=0)
        spot = jnp.int32(0)
        for k in range(slots):
            spot = jnp.where(perm[0, k] == s, k, spot)
        gather = jnp.where(
            iota((cols, slots * cw), 1) == spot * cw + (iota((cols, slots * cw), 0) >> 2), 1.0 / 16.0, 0.0
        )
        return pooled + jnp.dot(summed, gather, precision=HIGHEST, preferred_element_type=F32)

    pooled = lax.fori_loop(0, slots, one_slot, jnp.zeros((mu, slots * cw), F32))
    cr = rows // 4
    m, q = iota((cr * half, mu), 0), iota((cr * half, mu), 1)
    rowsum = jnp.where(((m % half) == (q >> 4)) & ((m // half) == ((q & (rows - 1)) >> 2)), 1.0, 0.0)
    parts[me] = jnp.dot(rowsum, pooled, precision=HIGHEST, preferred_element_type=F32)

    copies = []
    for d in range(1, npeer):
        peer = lax.rem(me + d, npeer)
        copy = pltpu.make_async_remote_copy(
            parts.at[me], parts.at[me], pool_send.at[d - 1], pool_recv.at[d - 1],
            device_id={"band": peer // nr, "rep": lax.rem(peer, nr)}, device_id_type=MESH,
        )
        copy.start()
        copies.append(copy)
    held = csl[...]
    pre = jnp.dot(u_state[...], held, precision=HIGHEST, preferred_element_type=F32) + coarse_bias
    for copy in copies:
        copy.wait()
    halves = []
    for r in range(nr):
        total = parts[r]
        for b in range(1, nb):
            total = total + parts[b * nr + r]
        halves.append(pltpu.roll(total, lax.rem(slots * cw - band * (own * cw), slots * cw), 1))
    wide = jnp.concatenate(
        [jnp.concatenate([x[i * half : (i + 1) * half] for x in halves], axis=0) for i in range(cr)], axis=1
    )
    pre = pre + jnp.dot(u_pool[...], wide, precision=HIGHEST, preferred_element_type=F32)
    new = held + jnp.tanh(pre)
    for k in range(own):
        for i in range(cr):
            cout[k, :, i, :] = new[:, i * cols + k * cw : i * cols + (k + 1) * cw]


def shards(nt, nb, nr, features, state, live, nbrs, perm, cs, wu, bu, wr, br, wc, bc, u_pool, u_state, b_coarse):
    bands, slots, chans, rows, cols = state.shape
    width = features.shape[2] + chans
    half = chans // nr
    km, kh = width * rows, width * 8
    kt = 3 * (km + 2 * kh)
    cr = rows // 4
    vm = pl.BlockSpec(memory_space=pltpu.VMEM)
    sm = pl.BlockSpec(memory_space=pltpu.SMEM)
    return pl.pallas_call(
        functools.partial(kernel, nt, nb, nr),
        out_shape=(
            jax.ShapeDtypeStruct((bands, slots, half, rows, cols), F32),
            jax.ShapeDtypeStruct(cs.shape, F32),
        ),
        in_specs=[vm, vm, sm, sm, sm, vm, vm, sm, vm, sm, vm, sm, vm, vm, sm],
        out_specs=(vm, vm),
        scratch_shapes=[
            pltpu.VMEM((slots, bands, km, cols), BF16),
            pltpu.VMEM((slots + 2, bands, kh, cols), BF16),
            pltpu.VMEM((slots + 2, bands, kh, cols), BF16),
            pltpu.VMEM((bands, kh, cols), BF16),
            pltpu.VMEM((bands, kh, cols), BF16),
            pltpu.VMEM((9, chans, kt), F32),
            pltpu.VMEM((half * rows + chans * (rows + 16), kt), BF16),
            pltpu.VMEM((half * rows, kt), BF16),
            pltpu.VMEM((kt, bands * cols), BF16),
            pltpu.VMEM((kt, bands * cols), BF16),
            pltpu.VMEM((nb * nr, cr * half, cols), F32),
            pltpu.VMEM((chans, cr * cols), F32),
            pltpu.SemaphoreType.DMA((2,)),
            pltpu.SemaphoreType.DMA((2,)),
            pltpu.SemaphoreType.DMA((nb * nr - 1,)),
            pltpu.SemaphoreType.DMA((nb * nr - 1,)),
        ],
        compiler_params=pltpu.CompilerParams(
            collective_id=0, has_side_effects=True, vmem_limit_bytes=40 * 1024 * 1024
        ),
    )(features, state, live, nbrs, perm, cs, wu, bu, wr, br, wc, bc, u_pool, u_state, b_coarse)


def solution(mesh):
    nt, nb, nr = mesh.shape["tiles"], mesh.shape["band"], mesh.shape["rep"]
    return jax.shard_map(
        functools.partial(shards, nt, nb, nr),
        mesh=mesh,
        in_specs=(
            P(("groups", "band"), "tiles", None, None, None),
            P(("groups", "band"), "tiles", None, None, None),
            P("tiles"),
            P("tiles", None),
            P("tiles", None),
            P(("groups", "tiles", "band"), None, None, None),
            P(),
            P(),
            P(),
            P(),
            P(),
            P(),
            P(),
            P(),
            P(),
        ),
        out_specs=(
            P(("groups", "band"), "tiles", "rep", None, None),
            P(("groups", "tiles", "band"), None, None, None),
        ),
        check_vma=False,
    )
```

time: 66.3 us -> 28.6 us (0.43)
  Pallas kernels: 0 us -> 18.5 us
  between operations: 14.4 us -> 0.73 us
  waiting for transfers between devices: 10.9 us -> 0 us
  matrix products: 10.7 us -> 0 us
  other arithmetic: 8.41 us -> 0 us
  starting transfers between devices: 6.89 us -> 0 us
  blocking collectives: 4.73 us -> 0 us
  local copies, waits for them, and re-layouts: 9.87 us -> 8.84 us
    pallas_call x0 -> x1, Pallas kernels: none -> 18.5 us  [shards(): pl.pallas_call(functools.partial(kernel, nt, nb, nr), out_shape=(jax.Shap...]
    reduce_scatter x1 -> x0, waiting for transfers between devices: 10.9 us -> none  [shards(): owned = lax.psum_scatter(ordered, 'band', scatter_dimension=0, tiled=True)]
    dot_general x29 -> x0, matrix products: 10.7 us -> none  [the longest x27 10.3 us: apply_filter(): jnp.einsum('oi,bsirw->bsorw', filter_weight[(left_operand + 1) * 3 + (rig...]
    ppermute x2 -> x0, starting transfers between devices: 6.85 us -> none  [the longest x1 5.56 us: padded(): lax.ppermute(lax.slice_in_dim(block, block.shape[dim] - width, None, axis...]
    all_gather x2 -> x0, blocking collectives: 4.73 us -> none  [the longest x1 2.46 us: shards(): lax.all_gather((reset_half * wide_half.astype(jnp.float32)).astype(jnp.bf...]
    unnamed x29 -> x31, local copies, waits for them, and re-layouts: 4.41 us -> 8.84 us
    reduce_sum x2 -> x0, other arithmetic: 3.74 us -> none  [the longest x1 3.57 us: shards(): pooled = jnp.sum(jnp.sum(blocks, axis=(4, 6)), axis=0) / 16.0]
    reduce_sum x2 -> x0, local copies, waits for them, and re-layouts: 2.71 us -> none  [shards(): pooled = jnp.sum(jnp.sum(blocks, axis=(4, 6)), axis=0) / 16.0]
  transfers between devices with their start and end apart: 3 -> 0, of which waited for: 1 -> 0; matrix products, arithmetic and copies ran while one was open for 5% -> 0% of each run, Pallas kernels for 0% -> 0%
where the time goes in v1:
time: 28.6 us; the launch traced here: 28.1 us
  Pallas kernels  18.5 us (65%)
  local copies, waits for them, and re-layouts  8.84 us (31%)
  between operations  0.73 us (3%)
    pallas_call x1, Pallas kernels, shards(): pl.pallas_call(functools.partial(kernel, nt, nb, nr), out_shape=(jax.Shap...  18.5 us
    unnamed x31, local copies, waits for them, and re-layouts  8.84 us

profile of v1, /device:TPU:0, one launch (start us, length us, event | category | flops | bytes accessed | tf_op | source)
XLA Modules:
  0.0 28.1 jit_solution(18265706261701651373)
XLA Ops:
  0.6 0.0 copy-start.13
  0.6 0.0 copy-start.12
  0.7 0.0 copy-start.11
  0.7 0.0 copy-start.10
  0.7 0.0 copy-start.9
  0.7 0.0 copy-start.8
  0.7 0.8 %copy.17.nbrs = s32[4,2]{1,0:T(4,128)S(1)} copy(s32[4,2]{0,1:T(2,128)} %param.18) | data formatting | bytes 64 | tf_op args[3]
  1.5 0.0 copy-done.13
  1.5 0.0 copy-done.12
  1.5 0.0 copy-done.11
  1.5 0.0 copy-done.10
  1.5 0.0 copy-done.9
  1.5 0.0 copy-done.8
  1.5 0.0 copy-start
  1.5 1.2 %copy-done = f32[2,4,16,16,128]{4,3,2,1,0:T(8,128)S(1)} copy-done((f32[2,4,16,16,128]{4,3,2,1,0:T(8,128)S(1)}, f32[2,4,16,16,128]{4,3,2,1,0:T(8,128)}, u32[]{:S(2)}) %copy-start) | copy-done | bytes 1048600
  2.8 0.0 copy-start.1
  2.8 0.8 %copy-done.1 = bf16[2,4,2,16,128]{4,3,2,1,0:T(8,128)(2,1)S(1)} copy-done((bf16[2,4,2,16,128]{4,3,2,1,0:T(8,128)(2,1)S(1)}, bf16[2,4,2,16,128]{4,3,2,1,0:T(8,128)(2,1)}, u32[]{:S(2)}) %copy-start.1) | copy-done | bytes 65560
  3.6 0.0 copy-start.2
  3.6 0.8 %copy-done.2 = f32[2,16,4,32]{3,2,1,0:T(4,128)S(1)} copy-done((f32[2,16,4,32]{3,2,1,0:T(4,128)S(1)}, f32[2,16,4,32]{3,2,1,0:T(4,128)}, u32[]{:S(2)}) %copy-start.2) | copy-done | bytes 16408
  4.4 0.0 copy-start.3
  4.4 0.8 %copy-done.3 = bf16[9,16,18]{2,1,0:T(8,128)(2,1)S(1)} copy-done((bf16[9,16,18]{2,1,0:T(8,128)(2,1)S(1)}, bf16[9,16,18]{2,1,0:T(8,128)(2,1)}, u32[]{:S(2)}) %copy-start.3) | copy-done | bytes 5208
  5.2 0.0 copy-start.4
  5.2 0.8 %copy-done.4 = bf16[9,16,18]{2,1,0:T(8,128)(2,1)S(1)} copy-done((bf16[9,16,18]{2,1,0:T(8,128)(2,1)S(1)}, bf16[9,16,18]{2,1,0:T(8,128)(2,1)}, u32[]{:S(2)}) %copy-start.4) | copy-done | bytes 5208
  6.0 0.0 copy-start.5
  6.0 0.8 %copy-done.5 = bf16[9,16,18]{2,1,0:T(8,128)(2,1)S(1)} copy-done((bf16[9,16,18]{2,1,0:T(8,128)(2,1)S(1)}, bf16[9,16,18]{2,1,0:T(8,128)(2,1)}, u32[]{:S(2)}) %copy-start.5) | copy-done | bytes 5208
  6.7 0.0 copy-start.6
  6.7 0.7 %copy-done.6 = f32[16,16]{1,0:T(8,128)S(1)} copy-done((f32[16,16]{1,0:T(8,128)S(1)}, f32[16,16]{1,0:T(8,128)}, u32[]{:S(2)}) %copy-start.6) | copy-done | bytes 1048
  7.4 0.0 copy-start.7
  7.4 0.7 %copy-done.7 = f32[16,16]{1,0:T(8,128)S(1)} copy-done((f32[16,16]{1,0:T(8,128)S(1)}, f32[16,16]{1,0:T(8,128)}, u32[]{:S(2)}) %copy-start.7) | copy-done | bytes 1048
  8.1 18.5 %shard_map.158 = (f32[2,4,8,16,128]{4,3,2,1,0:T(8,128)S(1)}, f32[2,16,4,32]{3,2,1,0:T(4,128)S(1)}) custom-call(bf16[2,4,2,16,128]{4,3,2,1,0:T(8,128)(2,1)S(1)} %copy-done.1, f32[2,4,16,16,128]{4,3,2,1,0:T(8,128)S(1)} %copy-done, s32[4]{0:T(128)S(1)} %copy-done.8, s32[4,2]{1,0:T(4,128)S(1)} %copy.17.nbrs, s32[1,4]{1,0:T(1,128)S(1)} %copy-done.9, ...), custom_call_target="tpu_custom_call" | custom-call | tf_op jit(solution)/shard_map/pallas_call | solution.py:305
  26.7 0.8 %copy.20 = f32[2,4,8,16,128]{4,3,2,1,0:T(8,128)} copy(f32[2,4,8,16,128]{4,3,2,1,0:T(8,128)S(1)} %get-tuple-element.4) | data formatting | bytes 1048576
  27.5 0.6 %copy.21 = f32[2,16,4,32]{3,2,1,0:T(4,128)} copy(f32[2,16,4,32]{3,2,1,0:T(4,128)S(1)} %get-tuple-element.5) | data formatting | bytes 32768
Async XLA Ops:
  0.6 0.9 %copy-start.13 = (f32[16]{0:T(128)S(1)}, f32[16]{0:T(128)}, u32[]{:S(2)}) copy-start(f32[16]{0:T(128)} %b_coarse.1) | copy-start | bytes 196
  0.6 0.9 %copy-start.12 = (f32[16]{0:T(128)S(1)}, f32[16]{0:T(128)}, u32[]{:S(2)}) copy-start(f32[16]{0:T(128)} %bc.1) | copy-start | bytes 196
  0.7 0.8 %copy-start.11 = (f32[16]{0:T(128)S(1)}, f32[16]{0:T(128)}, u32[]{:S(2)}) copy-start(f32[16]{0:T(128)} %br.1) | copy-start | bytes 196
  0.7 0.8 %copy-start.10 = (f32[16]{0:T(128)S(1)}, f32[16]{0:T(128)}, u32[]{:S(2)}) copy-start(f32[16]{0:T(128)} %bu.1) | copy-start | bytes 196
  0.7 0.8 %copy-start.9 = (s32[1,4]{1,0:T(1,128)S(1)}, s32[1,4]{1,0:T(1,128)}, u32[]{:S(2)}) copy-start(s32[1,4]{1,0:T(1,128)} %perm.1) | copy-start | bytes 52
  0.7 0.8 %copy-start.8 = (s32[4]{0:T(128)S(1)}, s32[4]{0:T(128)}, u32[]{:S(2)}) copy-start(s32[4]{0:T(128)} %live.1) | copy-start | bytes 52
  1.5 1.2 %copy-start = (f32[2,4,16,16,128]{4,3,2,1,0:T(8,128)S(1)}, f32[2,4,16,16,128]{4,3,2,1,0:T(8,128)}, u32[]{:S(2)}) copy-start(f32[2,4,16,16,128]{4,3,2,1,0:T(8,128)} %state.1) | copy-start | bytes 3145732
  2.8 0.8 %copy-start.1 = (bf16[2,4,2,16,128]{4,3,2,1,0:T(8,128)(2,1)S(1)}, bf16[2,4,2,16,128]{4,3,2,1,0:T(8,128)(2,1)}, u32[]{:S(2)}) copy-start(bf16[2,4,2,16,128]{4,3,2,1,0:T(8,128)(2,1)} %features.1) | copy-start | bytes 196612
  3.6 0.8 %copy-start.2 = (f32[2,16,4,32]{3,2,1,0:T(4,128)S(1)}, f32[2,16,4,32]{3,2,1,0:T(4,128)}, u32[]{:S(2)}) copy-start(f32[2,16,4,32]{3,2,1,0:T(4,128)} %cs.1) | copy-start | bytes 49156
  4.4 0.8 %copy-start.3 = (bf16[9,16,18]{2,1,0:T(8,128)(2,1)S(1)}, bf16[9,16,18]{2,1,0:T(8,128)(2,1)}, u32[]{:S(2)}) copy-start(bf16[9,16,18]{2,1,0:T(8,128)(2,1)} %wu.1) | copy-start | bytes 15556
  5.2 0.8 %copy-start.4 = (bf16[9,16,18]{2,1,0:T(8,128)(2,1)S(1)}, bf16[9,16,18]{2,1,0:T(8,128)(2,1)}, u32[]{:S(2)}) copy-start(bf16[9,16,18]{2,1,0:T(8,128)(2,1)} %wr.1) | copy-start | bytes 15556
  6.0 0.8 %copy-start.5 = (bf16[9,16,18]{2,1,0:T(8,128)(2,1)S(1)}, bf16[9,16,18]{2,1,0:T(8,128)(2,1)}, u32[]{:S(2)}) copy-start(bf16[9,16,18]{2,1,0:T(8,128)(2,1)} %wc.1) | copy-start | bytes 15556
  6.7 0.7 %copy-start.6 = (f32[16,16]{1,0:T(8,128)S(1)}, f32[16,16]{1,0:T(8,128)}, u32[]{:S(2)}) copy-start(f32[16,16]{1,0:T(8,128)} %u_pool.1) | copy-start | bytes 3076
  7.4 0.7 %copy-start.7 = (f32[16,16]{1,0:T(8,128)S(1)}, f32[16,16]{1,0:T(8,128)}, u32[]{:S(2)}) copy-start(f32[16,16]{1,0:T(8,128)} %u_state.1) | copy-start | bytes 3076

commit v2 on v1

v2 whole, which is shorter than its diff:
```python
import functools

import jax
import jax.numpy as jnp
from jax import lax
from jax.experimental import pallas as pl
from jax.experimental.pallas import tpu as pltpu
from jax.sharding import PartitionSpec as P

MESH = pl.DeviceIdType.MESH
HIGHEST = lax.Precision.HIGHEST
F32 = jnp.float32
BF16 = jnp.bfloat16


def iota(shape, dim):
    return lax.broadcasted_iota(jnp.int32, shape, dim)


def sigmoid(x):
    return 0.5 * jnp.tanh(0.5 * x) + 0.5


def shifted(x, step):
    width = x.shape[1]
    wide = pltpu.roll(x, (-step) % width, 1)
    column = iota(x.shape, 1) + step
    return jnp.where((column >= 0) & (column < width), wide, jnp.zeros_like(wide))


def kernel(
    nt, nb, nr, ins, rows,
    live, nbrs, perm, bu, br, bc, b_coarse, features_in, state_in, cs_in, wu_in, wr_in, wc_in, u_pool_in, u_state_in,
    out, cout,
    features, state, cs, wu, wr, wc, u_pool, u_state,
    feats, send_up, send_dn, got_up, got_dn, tops, bots, gtops, gbots, strip, gates,
    w1, w2, w3, t1, t2, t3, x1, x2, parts, csl,
    load_sems, up_sems, dn_sems, pool_send, pool_recv,
):
    bands, slots, flat, cols = state.shape
    chans = flat // rows
    half = chans // nr
    width = ins + chans
    own, cr, cw = cs.shape[0], cs.shape[2], cs.shape[3]
    km = width * rows
    slab = strip.shape[0] // 12
    tile = lax.axis_index("tiles")
    band = lax.axis_index("band")
    rep = lax.axis_index("rep")
    base = tile * slots
    npeer = nb * nr
    me = band * nr + rep
    start = rep * half

    loads = [
        pltpu.make_async_copy(src, dst, load_sems.at[i])
        for i, (src, dst) in enumerate(
            (
                (state_in, state), (features_in, features), (wu_in, wu), (wr_in, wr), (wc_in, wc),
                (cs_in, cs), (u_pool_in, u_pool), (u_state_in, u_state),
            )
        )
    ]
    for load in loads:
        load.start()

    barrier = pltpu.get_barrier_semaphore()
    has_up, has_dn = tile > 0, tile < nt - 1

    @pl.when(has_up)
    def _():
        pl.semaphore_signal(barrier, inc=1, device_id={"tiles": tile - 1}, device_id_type=MESH)

    @pl.when(has_dn)
    def _():
        pl.semaphore_signal(barrier, inc=1, device_id={"tiles": tile + 1}, device_id_type=MESH)

    for d in range(1, npeer):
        peer = lax.rem(me + d, npeer)
        pl.semaphore_signal(
            barrier, inc=1, device_id={"band": peer // nr, "rep": lax.rem(peer, nr)}, device_id_type=MESH
        )

    first = jnp.int32(0)
    last = jnp.int32(0)
    for s in range(slots):
        u, d = nbrs[0, s], nbrs[1, s]
        alive = live[s] > 0
        first = jnp.where(alive & ((u < base) | (u >= base + slots)), s, first)
        last = jnp.where(alive & ((d < base) | (d >= base + slots)), s, last)

    loads[0].wait()
    loads[1].wait()
    for s in range(slots):
        for b in range(bands):
            feats[b, s] = features[b, s].astype(F32)

    blank = jnp.zeros((slab - width, cols), F32)

    def feat_rows(b, s, row):
        return jnp.concatenate([feats[b, s, ch * rows + row : ch * rows + row + 1] for ch in range(ins)] + [blank], axis=0)

    def row_slab(b, s, row):
        return jnp.concatenate([state[b, s, pl.ds(row, chans, stride=rows), :], feat_rows(b, s, row)], axis=0).astype(BF16)

    for b in range(bands):
        for i in range(3):
            send_up[b, i] = row_slab(b, first, i)
            send_dn[b, i] = row_slab(b, last, rows - 3 + i)

    pl.semaphore_wait(barrier, npeer - 1 + jnp.where(has_up, 1, 0) + jnp.where(has_dn, 1, 0))

    def copy_up():
        return pltpu.make_async_remote_copy(
            send_up, got_dn, up_sems.at[0], up_sems.at[1], device_id={"tiles": tile - 1}, device_id_type=MESH
        )

    def copy_dn():
        return pltpu.make_async_remote_copy(
            send_dn, got_up, dn_sems.at[0], dn_sems.at[1], device_id={"tiles": tile + 1}, device_id_type=MESH
        )

    @pl.when(has_up)
    def _():
        copy_up().start()

    @pl.when(has_dn)
    def _():
        copy_dn().start()

    @pl.when(jnp.logical_not(has_up))
    def _():
        got_up[...] = jnp.zeros_like(got_up)

    @pl.when(jnp.logical_not(has_dn))
    def _():
        got_dn[...] = jnp.zeros_like(got_dn)

    def lanes(shape, main, halo):
        size = main + slab * len(halo)
        k = iota(shape, 1)
        side = (k >= size).astype(jnp.int32) + (k >= 2 * size).astype(jnp.int32)
        q = k - size * side
        h = q - main
        chan = jnp.where(h >= 0, h & (slab - 1), q >> 4)
        row = q & (rows - 1)
        for j, at in enumerate(halo):
            row = jnp.where(h >= j * slab, at, row)
        entry = jnp.where(chan < chans, chan + ins, chan - chans)
        return side, jnp.where(chan < width, entry, -1), row

    def spread(target, weights, main, halo):
        shape = (width, target.shape[2])
        side, entry, _ = lanes(shape, main, halo)
        total = jnp.zeros((3 * chans * len(weights), shape[1]), F32)
        for b in range(3):
            stack = jnp.concatenate([w[3 * a + b] for w in weights for a in range(3)], axis=0)
            pick = ((side == b) & (entry == iota(shape, 0))).astype(F32).astype(BF16)
            total = total + jnp.dot(stack, pick, preferred_element_type=F32)
        target[...] = total.reshape(target.shape)

    def fill(target, at, source, gate, outs, count, main, halo, dilation):
        shape = (rows, target.shape[1])
        _, _, row = lanes(shape, main, halo)
        delta = row - iota(shape, 0)
        hits = [(delta == a * dilation).astype(F32).astype(BF16) for a in (-1, 0, 1)]

        def step(o, carry):
            total = None
            for a in range(3):
                line = jnp.broadcast_to(source[3 * gate + a, pl.ds(outs + o, 1), :], shape).astype(BF16)
                total = line * hits[a] if total is None else total + line * hits[a]
            target[pl.ds(pl.multiple_of(at + o * rows, rows), rows), :] = total
            return carry

        lax.fori_loop(0, count, step, 0)

    mu = half * rows
    halo1, halo2, halo3 = (-1, rows), (-2, -1, rows, rows + 1), (-3, -2, -1, 0)
    for load in loads[2:5]:
        load.wait()
    spread(w1, (wu, wr), km, halo1)
    spread(w2, (wc,), km, halo2)
    spread(w3, (wr,), 0, halo3)
    fill(t1, 0, w1, 0, start, half, km, halo1, 1)
    fill(t1, mu, w1, 1, 0, chans, km, halo1, 1)
    fill(t2, 0, w2, 0, start, half, km, halo2, 2)
    _, _, row3 = lanes((chans, t3.shape[1]), 0, halo3)
    for i in range(2):
        total = jnp.zeros((chans, t3.shape[1]), F32)
        for a in range(3):
            total = jnp.where(row3 == i - 2 + a - 1, w3[a], total)
        t3[i * chans : (i + 1) * chans] = total.astype(BF16)

    for load in loads[5:]:
        load.wait()
    csl[...] = jnp.zeros_like(csl)
    for k in range(own):
        for i in range(cr):
            csl[:, i * cols + k * cw : i * cols + (k + 1) * cw] = cs[k, :, i, :]
    coarse_bias = jnp.zeros((chans, 1), F32)
    for o in range(chans):
        coarse_bias = jnp.where(iota((chans, 1), 0) == o, b_coarse[o], coarse_bias)

    k1, k2 = km + 2 * slab, km + 4 * slab
    for s in range(slots):
        for b in range(bands):
            at = slice(b * cols, (b + 1) * cols)
            tops[s, b] = row_slab(b, s, 0)
            bots[s, b] = row_slab(b, s, rows - 1)
            x = state[b, s].astype(BF16)
            f = features[b, s]
            for j, step in enumerate((-1, 0, 1)):
                x1[s, j * k1 : j * k1 + flat, at] = shifted(x, step) if step else x
                x1[s, j * k1 + flat : j * k1 + km, at] = shifted(f, step) if step else f
                x2[s, j * k2 + flat : j * k2 + km, at] = shifted(f, 2 * step) if step else f
    tops[slots + 1] = jnp.zeros((bands, slab, cols), BF16)
    bots[slots + 1] = jnp.zeros((bands, slab, cols), BF16)
    gtops[slots + 1] = jnp.zeros((bands, 2, slab, cols), BF16)
    gbots[slots + 1] = jnp.zeros((bands, 2, slab, cols), BF16)
    edge_up = [row_slab(b, first, 0) for b in range(bands)]
    edge_dn = [row_slab(b, last, rows - 1) for b in range(bands)]

    @pl.when(has_up)
    def _():
        copy_up().wait_send()

    @pl.when(has_dn)
    def _():
        copy_up().wait_recv()

    @pl.when(has_dn)
    def _():
        copy_dn().wait_send()

    @pl.when(has_up)
    def _():
        copy_dn().wait_recv()

    for b in range(bands):
        bots[slots, b] = got_up[b, 2]
        tops[slots, b] = got_dn[b, 0]
        for side in range(2):
            four = [got_up[b, i] for i in range(3)] + [edge_up[b]] if side == 0 else [edge_dn[b]] + [got_dn[b, i] for i in range(3)]
            at = slice((2 * side + b) * cols, (2 * side + b + 1) * cols)
            x = jnp.concatenate(four, axis=0)
            strip[0 : 4 * slab, at] = shifted(x, -1)
            strip[4 * slab : 8 * slab, at] = x
            strip[8 * slab :, at] = shifted(x, 1)
    acc = jnp.dot(t3[...], strip[...], preferred_element_type=F32)
    reset_bias = jnp.zeros((chans, 1), F32)
    for o in range(chans):
        reset_bias = jnp.where(iota((chans, 1), 0) == o, br[o], reset_bias)
    for b in range(bands):
        for side in range(2):
            at = slice((2 * side + b) * cols, (2 * side + b + 1) * cols)
            for i in range(2):
                held = (got_up[b, 1 + i] if side == 0 else got_dn[b, i]).astype(F32)
                reset = sigmoid(acc[i * chans : (i + 1) * chans, at] + reset_bias)
                joined = jnp.concatenate([reset * held[:chans], held[chans:]], axis=0).astype(BF16)
                if side == 0:
                    gbots[slots, b, i] = joined
                else:
                    gtops[slots, b, i] = joined

    def place(s, side):
        n = nbrs[side, s]
        here = (n >= base) & (n < base + slots)
        return jnp.where(here, n - base, jnp.where(n >= 0, slots, slots + 1))

    updates = []
    for s in range(slots):
        above, below = place(s, 0), place(s, 1)
        for b in range(bands):
            at = slice(b * cols, (b + 1) * cols)
            x = jnp.concatenate([bots[above, b], tops[below, b]], axis=0)
            for j, step in enumerate((-1, 0, 1)):
                x1[s, j * k1 + km : (j + 1) * k1, at] = shifted(x, step) if step else x
        acc = jnp.dot(t1[...], x1[s], preferred_element_type=F32)
        for b in range(bands):
            at = slice(b * cols, (b + 1) * cols)
            for o in range(half):
                gates[s, b, o * rows : (o + 1) * rows] = sigmoid(acc[o * rows : (o + 1) * rows, at] + bu[start + o])
            for o in range(chans):
                reset = sigmoid(acc[mu + o * rows : mu + (o + 1) * rows, at] + br[o])
                held = state[b, s, o * rows : (o + 1) * rows].astype(BF16).astype(F32)
                gates[s, b, mu + o * rows : mu + (o + 1) * rows] = reset * held
            x = gates[s, b, mu:].astype(BF16)
            for j, step in enumerate((-1, 0, 1)):
                x2[s, j * k2 : j * k2 + flat, at] = shifted(x, 2 * step) if step else x
            for i in range(2):
                for target, row in ((gtops, i), (gbots, rows - 2 + i)):
                    g = gates[s, b, pl.ds(mu + row, chans, stride=rows), :]
                    target[s, b, i] = jnp.concatenate([g, feat_rows(b, s, row)], axis=0).astype(BF16)

    pooled = jnp.zeros((mu, slots * cw), F32)
    for s in range(slots):
        above, below = place(s, 0), place(s, 1)
        for b in range(bands):
            at = slice(b * cols, (b + 1) * cols)
            x = jnp.concatenate([gbots[above, b, 0], gbots[above, b, 1], gtops[below, b, 0], gtops[below, b, 1]], axis=0)
            for j, step in enumerate((-1, 0, 1)):
                x2[s, j * k2 + km : (j + 1) * k2, at] = shifted(x, 2 * step) if step else x
        acc = jnp.dot(t2[...], x2[s], preferred_element_type=F32)
        scale = live[s].astype(F32)
        summed = []
        for o in range(half):
            both = None
            for b in range(bands):
                at = slice(b * cols, (b + 1) * cols)
                update = gates[s, b, o * rows : (o + 1) * rows]
                cand = jnp.tanh(acc[o * rows : (o + 1) * rows, at] + bc[start + o])
                held = state[b, s, pl.ds(pl.multiple_of((start + o) * rows, rows), rows), :]
                new = ((1.0 - update) * held + update * cand) * scale
                out[b, s, o] = new
                both = new if both is None else both + new
            summed.append(both)
        summed = jnp.concatenate(summed, axis=0)
        spot = jnp.int32(0)
        for k in range(slots):
            spot = jnp.where(perm[0, k] == s, k, spot)
        gather = jnp.where(
            iota((cols, slots * cw), 1) == spot * cw + (iota((cols, slots * cw), 0) >> 2), 1.0 / 16.0, 0.0
        )
        pooled = pooled + jnp.dot(summed, gather, precision=HIGHEST, preferred_element_type=F32)

    m, q = iota((cr * half, mu), 0), iota((cr * half, mu), 1)
    rowsum = jnp.where(((m % half) == (q >> 4)) & ((m // half) == ((q & (rows - 1)) >> 2)), 1.0, 0.0)
    parts[me] = jnp.dot(rowsum, pooled, precision=HIGHEST, preferred_element_type=F32)

    copies = []
    for d in range(1, npeer):
        peer = lax.rem(me + d, npeer)
        copy = pltpu.make_async_remote_copy(
            parts.at[me], parts.at[me], pool_send.at[d - 1], pool_recv.at[d - 1],
            device_id={"band": peer // nr, "rep": lax.rem(peer, nr)}, device_id_type=MESH,
        )
        copy.start()
        copies.append(copy)
    held = csl[...]
    pre = jnp.dot(u_state[...], held, precision=HIGHEST, preferred_element_type=F32) + coarse_bias
    for copy in copies:
        copy.wait()
    halves = []
    for r in range(nr):
        total = parts[r]
        for b in range(1, nb):
            total = total + parts[b * nr + r]
        halves.append(pltpu.roll(total, lax.rem(slots * cw - band * (own * cw), slots * cw), 1))
    wide = jnp.concatenate(
        [jnp.concatenate([x[i * half : (i + 1) * half] for x in halves], axis=0) for i in range(cr)], axis=1
    )
    pre = pre + jnp.dot(u_pool[...], wide, precision=HIGHEST, preferred_element_type=F32)
    new = held + jnp.tanh(pre)
    for k in range(own):
        for i in range(cr):
            cout[k, :, i, :] = new[:, i * cols + k * cw : i * cols + (k + 1) * cw]


def shards(nt, nb, nr, features, state, live, nbrs, perm, cs, wu, bu, wr, br, wc, bc, u_pool, u_state, b_coarse):
    bands, slots, chans, rows, cols = state.shape
    ins = features.shape[2]
    width = ins + chans
    half = chans // nr
    km = width * rows
    slab = 32
    k1, k2, k3 = 3 * (km + 2 * slab), 3 * (km + 4 * slab), 12 * slab
    cr = rows // 4
    hbm = pl.BlockSpec(memory_space=pl.ANY)
    vm = pl.BlockSpec(memory_space=pltpu.VMEM)
    sm = pl.BlockSpec(memory_space=pltpu.SMEM)
    features = features.reshape(bands, slots, ins * rows, cols)
    state = state.reshape(bands, slots, chans * rows, cols)
    big = (features, state, cs, wu, wr, wc, u_pool, u_state)
    return pl.pallas_call(
        functools.partial(kernel, nt, nb, nr, ins, rows),
        out_shape=(
            jax.ShapeDtypeStruct((bands, slots, half, rows, cols), F32),
            jax.ShapeDtypeStruct(cs.shape, F32),
        ),
        in_specs=[sm] * 7 + [hbm] * len(big),
        out_specs=(vm, vm),
        scratch_shapes=[pltpu.VMEM(x.shape, x.dtype) for x in big]
        + [
            pltpu.VMEM((bands, slots, ins * rows, cols), F32),
            pltpu.VMEM((bands, 3, slab, cols), BF16),
            pltpu.VMEM((bands, 3, slab, cols), BF16),
            pltpu.VMEM((bands, 3, slab, cols), BF16),
            pltpu.VMEM((bands, 3, slab, cols), BF16),
            pltpu.VMEM((slots + 2, bands, slab, cols), BF16),
            pltpu.VMEM((slots + 2, bands, slab, cols), BF16),
            pltpu.VMEM((slots + 2, bands, 2, slab, cols), BF16),
            pltpu.VMEM((slots + 2, bands, 2, slab, cols), BF16),
            pltpu.VMEM((k3, 2 * bands * cols), BF16),
            pltpu.VMEM((slots, bands, (half + chans) * rows, cols), F32),
            pltpu.VMEM((6, chans, k1), F32),
            pltpu.VMEM((3, chans, k2), F32),
            pltpu.VMEM((3, chans, k3), F32),
            pltpu.VMEM(((half + chans) * rows, k1), BF16),
            pltpu.VMEM((half * rows, k2), BF16),
            pltpu.VMEM((2 * chans, k3), BF16),
            pltpu.VMEM((slots, k1, bands * cols), BF16),
            pltpu.VMEM((slots, k2, bands * cols), BF16),
            pltpu.VMEM((nb * nr, cr * half, cols), F32),
            pltpu.VMEM((chans, cr * cols), F32),
            pltpu.SemaphoreType.DMA((len(big),)),
            pltpu.SemaphoreType.DMA((2,)),
            pltpu.SemaphoreType.DMA((2,)),
            pltpu.SemaphoreType.DMA((nb * nr - 1,)),
            pltpu.SemaphoreType.DMA((nb * nr - 1,)),
        ],
        compiler_params=pltpu.CompilerParams(
            collective_id=0, has_side_effects=True, vmem_limit_bytes=56 * 1024 * 1024
        ),
    )(live, nbrs.T, perm, bu, br, bc, b_coarse, *big)


def solution(mesh):
    nt, nb, nr = mesh.shape["tiles"], mesh.shape["band"], mesh.shape["rep"]
    return jax.shard_map(
        functools.partial(shards, nt, nb, nr),
        mesh=mesh,
        in_specs=(
            P(("groups", "band"), "tiles", None, None, None),
            P(("groups", "band"), "tiles", None, None, None),
            P("tiles"),
            P("tiles", None),
            P("tiles", None),
            P(("groups", "tiles", "band"), None, None, None),
            P(),
            P(),
            P(),
            P(),
            P(),
            P(),
            P(),
            P(),
            P(),
        ),
        out_specs=(
            P(("groups", "band"), "tiles", "rep", None, None),
            P(("groups", "tiles", "band"), None, None, None),
        ),
        check_vma=False,
    )
```

time: 28.6 us -> 18 us (0.63); the launches traced: 28.1 us -> 17.8 us
  local copies, waits for them, and re-layouts: 8.84 us -> 2.53 us
  Pallas kernels: 18.5 us -> 14.7 us
    unnamed x31 -> x4, local copies, waits for them, and re-layouts: 8.84 us -> 2.53 us
    pallas_call x1, Pallas kernels: 18.5 us -> 14.7 us  [shards(): pl.pallas_call(functools.partial(kernel, nt, nb, nr, ins, rows), out_shap...]
where the time goes in v2:
time: 18 us; the launch traced here: 17.8 us
  Pallas kernels  14.7 us (82%)
  local copies, waits for them, and re-layouts  2.53 us (14%)
  between operations  0.65 us (4%)
    pallas_call x1, Pallas kernels, shards(): pl.pallas_call(functools.partial(kernel, nt, nb, nr, ins, rows), out_shap...  14.7 us
    unnamed x4, local copies, waits for them, and re-layouts  2.53 us

profile of v2, /device:TPU:0, one launch (start us, length us, event | category | flops | bytes accessed | tf_op | source)
XLA Modules:
  0.0 17.8 jit_solution(9036107073921937425)
XLA Ops:
  0.6 14.7 %shard_map.158 = (f32[2,4,8,16,128]{4,3,2,1,0:T(8,128)}, f32[2,16,4,32]{3,2,1,0:T(4,128)}) custom-call(s32[4]{0:T(128)} %live.1, s32[2,4]{1,0:T(2,128)} %bitcast.5, s32[1,4]{1,0:T(1,128)} %perm.1, f32[16]{0:T(128)} %bu.1, f32[16]{0:T(128)} %br.1, f32[16]{0:T(128)} %bc.1, f32[16]{0:T(128)} %b_coarse.1, bf16[2,4,32,128]{3,2,1,0:T(8,128)(2,1)} %bitcast.4, ...), custom_call_target="tpu_custom_call" | custom-call | tf_op jit(solution)/shard_map/pallas_call | solution.py:375
  15.3 0.0 copy-start
  15.3 1.9 %copy.19 = f32[2,4,8,16,128]{4,3,2,1,0:T(8,128)} copy(f32[2,4,8,16,128]{4,3,2,1,0:T(8,128)} %get-tuple-element.4) | data formatting | bytes 1048576
  17.2 0.0 copy-done
  17.2 0.6 %copy.20 = f32[2,16,4,32]{3,2,1,0:T(4,128)} copy(f32[2,16,4,32]{3,2,1,0:T(4,128)S(1)} %copy-done) | data formatting | bytes 32768
Async XLA Ops:
  15.3 1.9 %copy-start = (f32[2,16,4,32]{3,2,1,0:T(4,128)S(1)}, f32[2,16,4,32]{3,2,1,0:T(4,128)}, u32[]{:S(2)}) copy-start(f32[2,16,4,32]{3,2,1,0:T(4,128)} %get-tuple-element.5) | copy-start | bytes 49156

commit v3 on v2

--- a/solution.py
+++ b/solution.py
@@ -30,12 +30,12 @@
 
 def kernel(
     nt, nb, nr, ins, rows,
-    live, nbrs, perm, bu, br, bc, b_coarse, features_in, state_in, cs_in, wu_in, wr_in, wc_in, u_pool_in, u_state_in,
-    out, cout,
-    features, state, cs, wu, wr, wc, u_pool, u_state,
+    live, nbrs, perm, bu, br, bc, b_coarse, features_in, state_in, cs_in, wu_in, wr_in, wc_in, u_state_in,
+    new_out, parts_out, coarse_out,
+    features, state, cs, wu, wr, wc, u_state, out, coarse,
     feats, send_up, send_dn, got_up, got_dn, tops, bots, gtops, gbots, strip, gates,
-    w1, w2, w3, t1, t2, t3, x1, x2, parts, csl,
-    load_sems, up_sems, dn_sems, pool_send, pool_recv,
+    w1, w2, w3, t1, t2, t3, x1, x2, part,
+    load_sems, up_sems, dn_sems, pool_send, pool_recv, store_sems,
 ):
     bands, slots, flat, cols = state.shape
     chans = flat // rows
@@ -56,8 +56,8 @@
         pltpu.make_async_copy(src, dst, load_sems.at[i])
         for i, (src, dst) in enumerate(
             (
-                (state_in, state), (features_in, features), (wu_in, wu), (wr_in, wr), (wc_in, wc),
-                (cs_in, cs), (u_pool_in, u_pool), (u_state_in, u_state),
+                (wu_in, wu), (wr_in, wr), (wc_in, wc), (features_in, features), (state_in, state),
+                (cs_in, cs), (u_state_in, u_state),
             )
         )
     ]
@@ -89,103 +89,99 @@
         first = jnp.where(alive & ((u < base) | (u >= base + slots)), s, first)
         last = jnp.where(alive & ((d < base) | (d >= base + slots)), s, last)
 
-    loads[0].wait()
-    loads[1].wait()
-    for s in range(slots):
-        for b in range(bands):
-            feats[b, s] = features[b, s].astype(F32)
-
-    blank = jnp.zeros((slab - width, cols), F32)
-
-    def feat_rows(b, s, row):
-        return jnp.concatenate([feats[b, s, ch * rows + row : ch * rows + row + 1] for ch in range(ins)] + [blank], axis=0)
-
-    def row_slab(b, s, row):
-        return jnp.concatenate([state[b, s, pl.ds(row, chans, stride=rows), :], feat_rows(b, s, row)], axis=0).astype(BF16)
-
-    for b in range(bands):
-        for i in range(3):
-            send_up[b, i] = row_slab(b, first, i)
-            send_dn[b, i] = row_slab(b, last, rows - 3 + i)
-
-    pl.semaphore_wait(barrier, npeer - 1 + jnp.where(has_up, 1, 0) + jnp.where(has_dn, 1, 0))
-
-    def copy_up():
-        return pltpu.make_async_remote_copy(
-            send_up, got_dn, up_sems.at[0], up_sems.at[1], device_id={"tiles": tile - 1}, device_id_type=MESH
-        )
-
-    def copy_dn():
-        return pltpu.make_async_remote_copy(
-            send_dn, got_up, dn_sems.at[0], dn_sems.at[1], device_id={"tiles": tile + 1}, device_id_type=MESH
-        )
-
-    @pl.when(has_up)
-    def _():
-        copy_up().start()
-
-    @pl.when(has_dn)
-    def _():
-        copy_dn().start()
-
-    @pl.when(jnp.logical_not(has_up))
-    def _():
-        got_up[...] = jnp.zeros_like(got_up)
-
-    @pl.when(jnp.logical_not(has_dn))
-    def _():
-        got_dn[...] = jnp.zeros_like(got_dn)
-
-    def lanes(shape, main, halo):
-        size = main + slab * len(halo)
-        k = iota(shape, 1)
-        side = (k >= size).astype(jnp.int32) + (k >= 2 * size).astype(jnp.int32)
-        q = k - size * side
+    def lanes(size, main, halo):
+        part = size // 3
+        k = iota((1, size), 1)
+        side = (k >= part).astype(jnp.int32) + (k >= 2 * part).astype(jnp.int32)
+        q = k - part * side
         h = q - main
         chan = jnp.where(h >= 0, h & (slab - 1), q >> 4)
         row = q & (rows - 1)
         for j, at in enumerate(halo):
             row = jnp.where(h >= j * slab, at, row)
         entry = jnp.where(chan < chans, chan + ins, chan - chans)
-        return side, jnp.where(chan < width, entry, -1), row
+        return jnp.where(chan < width, entry + 32 * side, -1), row
 
     def spread(target, weights, main, halo):
-        shape = (width, target.shape[2])
-        side, entry, _ = lanes(shape, main, halo)
-        total = jnp.zeros((3 * chans * len(weights), shape[1]), F32)
+        size = target.shape[2]
+        entry, _ = lanes(size, main, halo)
+        total = jnp.zeros((3 * chans * len(weights), size), F32)
         for b in range(3):
             stack = jnp.concatenate([w[3 * a + b] for w in weights for a in range(3)], axis=0)
-            pick = ((side == b) & (entry == iota(shape, 0))).astype(F32).astype(BF16)
+            pick = (entry == iota((width, size), 0) + 32 * b).astype(F32).astype(BF16)
             total = total + jnp.dot(stack, pick, preferred_element_type=F32)
         target[...] = total.reshape(target.shape)
 
-    def fill(target, at, source, gate, outs, count, main, halo, dilation):
+    def fill(target, source, jobs, main, halo, dilation):
         shape = (rows, target.shape[1])
-        _, _, row = lanes(shape, main, halo)
+        _, row = lanes(shape[1], main, halo)
         delta = row - iota(shape, 0)
         hits = [(delta == a * dilation).astype(F32).astype(BF16) for a in (-1, 0, 1)]
-
-        def step(o, carry):
-            total = None
-            for a in range(3):
-                line = jnp.broadcast_to(source[3 * gate + a, pl.ds(outs + o, 1), :], shape).astype(BF16)
-                total = line * hits[a] if total is None else total + line * hits[a]
-            target[pl.ds(pl.multiple_of(at + o * rows, rows), rows), :] = total
-            return carry
-
-        lax.fori_loop(0, count, step, 0)
+        for at, gate, outs, count in jobs:
+            for o in range(count):
+                total = None
+                for a in range(3):
+                    line = jnp.broadcast_to(source[3 * gate + a, pl.ds(outs + o, 1), :], shape).astype(BF16)
+                    total = line * hits[a] if total is None else total + line * hits[a]
+                target[at + o * rows : at + (o + 1) * rows, :] = total
 
     mu = half * rows
     halo1, halo2, halo3 = (-1, rows), (-2, -1, rows, rows + 1), (-3, -2, -1, 0)
-    for load in loads[2:5]:
+    for load in loads[:3]:
         load.wait()
     spread(w1, (wu, wr), km, halo1)
     spread(w2, (wc,), km, halo2)
     spread(w3, (wr,), 0, halo3)
-    fill(t1, 0, w1, 0, start, half, km, halo1, 1)
-    fill(t1, mu, w1, 1, 0, chans, km, halo1, 1)
-    fill(t2, 0, w2, 0, start, half, km, halo2, 2)
-    _, _, row3 = lanes((chans, t3.shape[1]), 0, halo3)
+    loads[3].wait()
+    loads[4].wait()
+    for s in range(slots):
+        for b in range(bands):
+            feats[b, s] = features[b, s].astype(F32)
+
+    blank = jnp.zeros((slab - width, cols), F32)
+
+    def feat_rows(b, s, row):
+        return jnp.concatenate([feats[b, s, ch * rows + row : ch * rows + row + 1] for ch in range(ins)] + [blank], axis=0)
+
+    def row_slab(b, s, row):
+        return jnp.concatenate([state[b, s, pl.ds(row, chans, stride=rows), :], feat_rows(b, s, row)], axis=0).astype(BF16)
+
+    for b in range(bands):
+        for i in range(3):
+            send_up[b, i] = row_slab(b, first, i)
+            send_dn[b, i] = row_slab(b, last, rows - 3 + i)
+
+    pl.semaphore_wait(barrier, npeer - 1 + jnp.where(has_up, 1, 0) + jnp.where(has_dn, 1, 0))
+
+    def copy_up():
+        return pltpu.make_async_remote_copy(
+            send_up, got_dn, up_sems.at[0], up_sems.at[1], device_id={"tiles": tile - 1}, device_id_type=MESH
+        )
+
+    def copy_dn():
+        return pltpu.make_async_remote_copy(
+            send_dn, got_up, dn_sems.at[0], dn_sems.at[1], device_id={"tiles": tile + 1}, device_id_type=MESH
+        )
+
+    @pl.when(has_up)
+    def _():
+        copy_up().start()
+
+    @pl.when(has_dn)
+    def _():
+        copy_dn().start()
+
+    @pl.when(jnp.logical_not(has_up))
+    def _():
+        got_up[...] = jnp.zeros_like(got_up)
+
+    @pl.when(jnp.logical_not(has_dn))
+    def _():
+        got_dn[...] = jnp.zeros_like(got_dn)
+
+    fill(t1, w1, ((0, 0, start, half), (mu, 1, 0, chans)), km, halo1, 1)
+    fill(t2, w2, ((0, 0, start, half),), km, halo2, 2)
+    _, row3 = lanes(t3.shape[1], 0, halo3)
     for i in range(2):
         total = jnp.zeros((chans, t3.shape[1]), F32)
         for a in range(3):
@@ -194,13 +190,16 @@
 
     for load in loads[5:]:
         load.wait()
-    csl[...] = jnp.zeros_like(csl)
+    coarse[0] = jnp.zeros_like(coarse[0])
     for k in range(own):
         for i in range(cr):
-            csl[:, i * cols + k * cw : i * cols + (k + 1) * cw] = cs[k, :, i, :]
+            coarse[0, :, i * cols + k * cw : i * cols + (k + 1) * cw] = cs[k, :, i, :]
     coarse_bias = jnp.zeros((chans, 1), F32)
     for o in range(chans):
         coarse_bias = jnp.where(iota((chans, 1), 0) == o, b_coarse[o], coarse_bias)
+    coarse[1] = jnp.dot(u_state[...], coarse[0], precision=HIGHEST, preferred_element_type=F32) + coarse_bias
+    stores = [pltpu.make_async_copy(coarse, coarse_out, store_sems.at[0])]
+    stores[0].start()
 
     k1, k2 = km + 2 * slab, km + 4 * slab
     for s in range(slots):
@@ -240,28 +239,6 @@
     for b in range(bands):
         bots[slots, b] = got_up[b, 2]
         tops[slots, b] = got_dn[b, 0]
-        for side in range(2):
-            four = [got_up[b, i] for i in range(3)] + [edge_up[b]] if side == 0 else [edge_dn[b]] + [got_dn[b, i] for i in range(3)]
-            at = slice((2 * side + b) * cols, (2 * side + b + 1) * cols)
-            x = jnp.concatenate(four, axis=0)
-            strip[0 : 4 * slab, at] = shifted(x, -1)
-            strip[4 * slab : 8 * slab, at] = x
-            strip[8 * slab :, at] = shifted(x, 1)
-    acc = jnp.dot(t3[...], strip[...], preferred_element_type=F32)
-    reset_bias = jnp.zeros((chans, 1), F32)
-    for o in range(chans):
-        reset_bias = jnp.where(iota((chans, 1), 0) == o, br[o], reset_bias)
-    for b in range(bands):
-        for side in range(2):
-            at = slice((2 * side + b) * cols, (2 * side + b + 1) * cols)
-            for i in range(2):
-                held = (got_up[b, 1 + i] if side == 0 else got_dn[b, i]).astype(F32)
-                reset = sigmoid(acc[i * chans : (i + 1) * chans, at] + reset_bias)
-                joined = jnp.concatenate([reset * held[:chans], held[chans:]], axis=0).astype(BF16)
-                if side == 0:
-                    gbots[slots, b, i] = joined
-                else:
-                    gtops[slots, b, i] = joined
 
     def place(s, side):
         n = nbrs[side, s]
@@ -293,6 +270,30 @@
                     g = gates[s, b, pl.ds(mu + row, chans, stride=rows), :]
                     target[s, b, i] = jnp.concatenate([g, feat_rows(b, s, row)], axis=0).astype(BF16)
 
+    for b in range(bands):
+        for side in range(2):
+            four = [got_up[b, i] for i in range(3)] + [edge_up[b]] if side == 0 else [edge_dn[b]] + [got_dn[b, i] for i in range(3)]
+            at = slice((2 * side + b) * cols, (2 * side + b + 1) * cols)
+            x = jnp.concatenate(four, axis=0)
+            strip[0 : 4 * slab, at] = shifted(x, -1)
+            strip[4 * slab : 8 * slab, at] = x
+            strip[8 * slab :, at] = shifted(x, 1)
+    acc = jnp.dot(t3[...], strip[...], preferred_element_type=F32)
+    reset_bias = jnp.zeros((chans, 1), F32)
+    for o in range(chans):
+        reset_bias = jnp.where(iota((chans, 1), 0) == o, br[o], reset_bias)
+    for b in range(bands):
+        for side in range(2):
+            at = slice((2 * side + b) * cols, (2 * side + b + 1) * cols)
+            for i in range(2):
+                held = (got_up[b, 1 + i] if side == 0 else got_dn[b, i]).astype(F32)
+                reset = sigmoid(acc[i * chans : (i + 1) * chans, at] + reset_bias)
+                joined = jnp.concatenate([reset * held[:chans], held[chans:]], axis=0).astype(BF16)
+                if side == 0:
+                    gbots[slots, b, i] = joined
+                else:
+                    gtops[slots, b, i] = joined
+
     pooled = jnp.zeros((mu, slots * cw), F32)
     for s in range(slots):
         above, below = place(s, 0), place(s, 1)
@@ -315,6 +316,8 @@
                 out[b, s, o] = new
                 both = new if both is None else both + new
             summed.append(both)
+        stores.append(pltpu.make_async_copy(out.at[:, s], new_out.at[:, s], store_sems.at[s + 1]))
+        stores[-1].start()
         summed = jnp.concatenate(summed, axis=0)
         spot = jnp.int32(0)
         for k in range(slots):
@@ -325,36 +328,60 @@
         pooled = pooled + jnp.dot(summed, gather, precision=HIGHEST, preferred_element_type=F32)
 
     m, q = iota((cr * half, mu), 0), iota((cr * half, mu), 1)
-    rowsum = jnp.where(((m % half) == (q >> 4)) & ((m // half) == ((q & (rows - 1)) >> 2)), 1.0, 0.0)
-    parts[me] = jnp.dot(rowsum, pooled, precision=HIGHEST, preferred_element_type=F32)
+    rowsum = jnp.where(((m & (half - 1)) == (q >> 4)) & ((m >> (half.bit_length() - 1)) == ((q & (rows - 1)) >> 2)), 1.0, 0.0)
+    part[...] = jnp.dot(rowsum, pooled, precision=HIGHEST, preferred_element_type=F32)
 
     copies = []
     for d in range(1, npeer):
         peer = lax.rem(me + d, npeer)
         copy = pltpu.make_async_remote_copy(
-            parts.at[me], parts.at[me], pool_send.at[d - 1], pool_recv.at[d - 1],
+            part, parts_out.at[me], pool_send.at[d - 1], pool_recv.at[d - 1],
             device_id={"band": peer // nr, "rep": lax.rem(peer, nr)}, device_id_type=MESH,
         )
         copy.start()
         copies.append(copy)
-    held = csl[...]
-    pre = jnp.dot(u_state[...], held, precision=HIGHEST, preferred_element_type=F32) + coarse_bias
-    for copy in copies:
+    stores.append(pltpu.make_async_copy(part, parts_out.at[me], store_sems.at[slots + 1]))
+    stores[-1].start()
+    for copy in stores + copies:
         copy.wait()
+
+
+def finish(
+    nb, nr, own, parts_in, coarse_in, u_pool_in, new_in, out, cout, parts, coarse, u_pool, load_sems, store_sems
+):
+    bands, slots, half = new_in.shape[:3]
+    cr, cw = cout.shape[2], cout.shape[3]
+    cols = slots * cw
+    band = lax.axis_index("band")
+    loads = [
+        pltpu.make_async_copy(src, dst, load_sems.at[i])
+        for i, (src, dst) in enumerate(((parts_in, parts), (coarse_in, coarse), (u_pool_in, u_pool)))
+    ]
+    for load in loads:
+        load.start()
+    stores = []
+    for b in range(bands):
+        for s in range(slots):
+            stores.append(pltpu.make_async_copy(new_in.at[b, s], out.at[b, s], store_sems.at[b * slots + s]))
+            stores[-1].start()
+    for load in loads:
+        load.wait()
     halves = []
     for r in range(nr):
         total = parts[r]
         for b in range(1, nb):
             total = total + parts[b * nr + r]
-        halves.append(pltpu.roll(total, lax.rem(slots * cw - band * (own * cw), slots * cw), 1))
+        halves.append(pltpu.roll(total, lax.rem(cols - band * (own * cw), cols), 1))
     wide = jnp.concatenate(
         [jnp.concatenate([x[i * half : (i + 1) * half] for x in halves], axis=0) for i in range(cr)], axis=1
     )
-    pre = pre + jnp.dot(u_pool[...], wide, precision=HIGHEST, preferred_element_type=F32)
-    new = held + jnp.tanh(pre)
+    pre = coarse[1] + jnp.dot(u_pool[...], wide, precision=HIGHEST, preferred_element_type=F32)
+    new = coarse[0] + jnp.tanh(pre)
     for k in range(own):
         for i in range(cr):
             cout[k, :, i, :] = new[:, i * cols + k * cw : i * cols + (k + 1) * cw]
+    for store in stores:
+        store.wait()
 
 
 def shards(nt, nb, nr, features, state, live, nbrs, perm, cs, wu, bu, wr, br, wc, bc, u_pool, u_state, b_coarse):
@@ -366,21 +393,21 @@
     slab = 32
     k1, k2, k3 = 3 * (km + 2 * slab), 3 * (km + 4 * slab), 12 * slab
     cr = rows // 4
-    hbm = pl.BlockSpec(memory_space=pl.ANY)
+    hbm = pl.BlockSpec(memory_space=pltpu.HBM)
     vm = pl.BlockSpec(memory_space=pltpu.VMEM)
     sm = pl.BlockSpec(memory_space=pltpu.SMEM)
     features = features.reshape(bands, slots, ins * rows, cols)
     state = state.reshape(bands, slots, chans * rows, cols)
-    big = (features, state, cs, wu, wr, wc, u_pool, u_state)
-    return pl.pallas_call(
+    big = (features, state, cs, wu, wr, wc, u_state)
+    fine = jax.ShapeDtypeStruct((bands, slots, half, rows, cols), F32)
+    pooled = jax.ShapeDtypeStruct((nb * nr, cr * half, cols), F32)
+    coarse = jax.ShapeDtypeStruct((2, chans, cr * cols), F32)
+    new, parts, held = pl.pallas_call(
         functools.partial(kernel, nt, nb, nr, ins, rows),
-        out_shape=(
-            jax.ShapeDtypeStruct((bands, slots, half, rows, cols), F32),
-            jax.ShapeDtypeStruct(cs.shape, F32),
-        ),
+        out_shape=(fine, pooled, coarse),
         in_specs=[sm] * 7 + [hbm] * len(big),
-        out_specs=(vm, vm),
-        scratch_shapes=[pltpu.VMEM(x.shape, x.dtype) for x in big]
+        out_specs=(hbm, hbm, hbm),
+        scratch_shapes=[pltpu.VMEM(x.shape, x.dtype) for x in big + (fine, coarse)]
         + [
             pltpu.VMEM((bands, slots, ins * rows, cols), F32),
             pltpu.VMEM((bands, 3, slab, cols), BF16),
@@ -401,18 +428,32 @@
             pltpu.VMEM((2 * chans, k3), BF16),
             pltpu.VMEM((slots, k1, bands * cols), BF16),
             pltpu.VMEM((slots, k2, bands * cols), BF16),
-            pltpu.VMEM((nb * nr, cr * half, cols), F32),
-            pltpu.VMEM((chans, cr * cols), F32),
+            pltpu.VMEM((cr * half, cols), F32),
             pltpu.SemaphoreType.DMA((len(big),)),
             pltpu.SemaphoreType.DMA((2,)),
             pltpu.SemaphoreType.DMA((2,)),
             pltpu.SemaphoreType.DMA((nb * nr - 1,)),
             pltpu.SemaphoreType.DMA((nb * nr - 1,)),
+            pltpu.SemaphoreType.DMA((slots + 2,)),
         ],
         compiler_params=pltpu.CompilerParams(
             collective_id=0, has_side_effects=True, vmem_limit_bytes=56 * 1024 * 1024
         ),
     )(live, nbrs.T, perm, bu, br, bc, b_coarse, *big)
+    return pl.pallas_call(
+        functools.partial(finish, nb, nr, cs.shape[0]),
+        out_shape=(fine, jax.ShapeDtypeStruct(cs.shape, F32)),
+        in_specs=[hbm] * 4,
+        out_specs=(hbm, vm),
+        scratch_shapes=[
+            pltpu.VMEM(pooled.shape, F32),
+            pltpu.VMEM(coarse.shape, F32),
+            pltpu.VMEM(u_pool.shape, F32),
+            pltpu.SemaphoreType.DMA((3,)),
+            pltpu.SemaphoreType.DMA((bands * slots,)),
+        ],
+        compiler_params=pltpu.CompilerParams(vmem_limit_bytes=56 * 1024 * 1024),
+    )(parts, held, u_pool, new)
 
 
 def solution(mesh):

time: 18 us -> 32.3 us (1.79)
  Pallas kernels: 14.7 us -> 31.4 us
  local copies, waits for them, and re-layouts: 2.53 us -> 0 us
    pallas_call x0 -> x1, Pallas kernels: none -> 17.7 us  [shards(): pl.pallas_call(functools.partial(finish, nb, nr, cs.shape[0]), out_shape=...]
    unnamed x4 -> x0, local copies, waits for them, and re-layouts: 2.53 us -> none
    pallas_call x1, Pallas kernels: 14.7 us -> 13.7 us  [shards(): pl.pallas_call(functools.partial(kernel, nt, nb, nr, ins, rows), out_shap...]
where the time goes in v3:
time: 32.3 us; the launch traced here: 32.1 us
  Pallas kernels  31.4 us (97%)
  between operations  0.64 us (2%)
    pallas_call x1, Pallas kernels, shards(): pl.pallas_call(functools.partial(finish, nb, nr, cs.shape[0]), out_shape=...  17.7 us
    pallas_call x1, Pallas kernels, shards(): pl.pallas_call(functools.partial(kernel, nt, nb, nr, ins, rows), out_shap...  13.7 us

profile of v3, /device:TPU:0, one launch (start us, length us, event | category | flops | bytes accessed | tf_op | source)
XLA Modules:
  0.0 32.1 jit_solution(14718660101320216826)
XLA Ops:
  0.6 13.7 %shard_map.158 = (f32[2,4,8,16,128]{4,3,2,1,0:T(8,128)}, f32[4,32,128]{2,1,0:T(8,128)}, f32[2,16,512]{2,1,0:T(8,128)}) custom-call(s32[4]{0:T(128)} %live.1, s32[2,4]{1,0:T(2,128)} %bitcast.5, s32[1,4]{1,0:T(1,128)} %perm.1, f32[16]{0:T(128)} %bu.1, f32[16]{0:T(128)} %br.1, f32[16]{0:T(128)} %bc.1, f32[16]{0:T(128)} %b_coarse.1, ...), custom_call_target="tpu_custom_call" | custom-call | tf_op jit(solution)/shard_map/pallas_call | solution.py:405
  14.3 17.7 %shard_map.159 = (f32[2,4,8,16,128]{4,3,2,1,0:T(8,128)}, f32[2,16,4,32]{3,2,1,0:T(4,128)}) custom-call(f32[4,32,128]{2,1,0:T(8,128)} %get-tuple-element.5.parts_in, f32[2,16,512]{2,1,0:T(8,128)} %get-tuple-element.6.coarse_in, f32[16,16]{1,0:T(8,128)} %u_pool_in.1, f32[2,4,8,16,128]{4,3,2,1,0:T(8,128)} %get-tuple-element.7.new_in), custom_call_target="tpu_custom_call" | custom-call | tf_op jit(solution)/shard_map/pallas_call | solution.py:443

commit v4 on v3

--- a/solution.py
+++ b/solution.py
@@ -31,11 +31,11 @@
 def kernel(
     nt, nb, nr, ins, rows,
     live, nbrs, perm, bu, br, bc, b_coarse, features_in, state_in, cs_in, wu_in, wr_in, wc_in, u_state_in,
-    new_out, parts_out, coarse_out,
-    features, state, cs, wu, wr, wc, u_state, out, coarse,
+    out, parts, coarse,
+    features, state, cs, wu, wr, wc, u_state,
     feats, send_up, send_dn, got_up, got_dn, tops, bots, gtops, gbots, strip, gates,
-    w1, w2, w3, t1, t2, t3, x1, x2, part,
-    load_sems, up_sems, dn_sems, pool_send, pool_recv, store_sems,
+    w1, w2, w3, t1, t2, t3, x1, x2,
+    load_sems, up_sems, dn_sems, pool_send, pool_recv,
 ):
     bands, slots, flat, cols = state.shape
     chans = flat // rows
@@ -198,8 +198,6 @@
     for o in range(chans):
         coarse_bias = jnp.where(iota((chans, 1), 0) == o, b_coarse[o], coarse_bias)
     coarse[1] = jnp.dot(u_state[...], coarse[0], precision=HIGHEST, preferred_element_type=F32) + coarse_bias
-    stores = [pltpu.make_async_copy(coarse, coarse_out, store_sems.at[0])]
-    stores[0].start()
 
     k1, k2 = km + 2 * slab, km + 4 * slab
     for s in range(slots):
@@ -316,8 +314,6 @@
                 out[b, s, o] = new
                 both = new if both is None else both + new
             summed.append(both)
-        stores.append(pltpu.make_async_copy(out.at[:, s], new_out.at[:, s], store_sems.at[s + 1]))
-        stores[-1].start()
         summed = jnp.concatenate(summed, axis=0)
         spot = jnp.int32(0)
         for k in range(slots):
@@ -329,43 +325,33 @@
 
     m, q = iota((cr * half, mu), 0), iota((cr * half, mu), 1)
     rowsum = jnp.where(((m & (half - 1)) == (q >> 4)) & ((m >> (half.bit_length() - 1)) == ((q & (rows - 1)) >> 2)), 1.0, 0.0)
-    part[...] = jnp.dot(rowsum, pooled, precision=HIGHEST, preferred_element_type=F32)
+    parts[me] = jnp.dot(rowsum, pooled, precision=HIGHEST, preferred_element_type=F32)
 
     copies = []
     for d in range(1, npeer):
         peer = lax.rem(me + d, npeer)
         copy = pltpu.make_async_remote_copy(
-            part, parts_out.at[me], pool_send.at[d - 1], pool_recv.at[d - 1],
+            parts.at[me], parts.at[me], pool_send.at[d - 1], pool_recv.at[d - 1],
             device_id={"band": peer // nr, "rep": lax.rem(peer, nr)}, device_id_type=MESH,
         )
         copy.start()
         copies.append(copy)
-    stores.append(pltpu.make_async_copy(part, parts_out.at[me], store_sems.at[slots + 1]))
-    stores[-1].start()
-    for copy in stores + copies:
+    for copy in copies:
         copy.wait()
 
 
 def finish(
-    nb, nr, own, parts_in, coarse_in, u_pool_in, new_in, out, cout, parts, coarse, u_pool, load_sems, store_sems
+    nb, nr, own, parts, coarse, u_pool, new_in, out, coarse_out, cout, store_sems
 ):
     bands, slots, half = new_in.shape[:3]
     cr, cw = cout.shape[2], cout.shape[3]
     cols = slots * cw
     band = lax.axis_index("band")
-    loads = [
-        pltpu.make_async_copy(src, dst, load_sems.at[i])
-        for i, (src, dst) in enumerate(((parts_in, parts), (coarse_in, coarse), (u_pool_in, u_pool)))
-    ]
-    for load in loads:
-        load.start()
     stores = []
     for b in range(bands):
         for s in range(slots):
             stores.append(pltpu.make_async_copy(new_in.at[b, s], out.at[b, s], store_sems.at[b * slots + s]))
             stores[-1].start()
-    for load in loads:
-        load.wait()
     halves = []
     for r in range(nr):
         total = parts[r]
@@ -380,6 +366,8 @@
     for k in range(own):
         for i in range(cr):
             cout[k, :, i, :] = new[:, i * cols + k * cw : i * cols + (k + 1) * cw]
+    stores.append(pltpu.make_async_copy(cout, coarse_out, store_sems.at[bands * slots]))
+    stores[-1].start()
     for store in stores:
         store.wait()
 
@@ -398,7 +386,12 @@
     sm = pl.BlockSpec(memory_space=pltpu.SMEM)
     features = features.reshape(bands, slots, ins * rows, cols)
     state = state.reshape(bands, slots, chans * rows, cols)
-    big = (features, state, cs, wu, wr, wc, u_state)
+    big = tuple(
+        pltpu.with_memory_space_constraint(x, pltpu.HBM) for x in (features, state, cs, wu, wr, wc, u_state)
+    )
+    small = tuple(
+        pltpu.with_memory_space_constraint(x, pltpu.HBM) for x in (live, nbrs.T, perm, bu, br, bc, b_coarse)
+    )
     fine = jax.ShapeDtypeStruct((bands, slots, half, rows, cols), F32)
     pooled = jax.ShapeDtypeStruct((nb * nr, cr * half, cols), F32)
     coarse = jax.ShapeDtypeStruct((2, chans, cr * cols), F32)
@@ -406,8 +399,8 @@
         functools.partial(kernel, nt, nb, nr, ins, rows),
         out_shape=(fine, pooled, coarse),
         in_specs=[sm] * 7 + [hbm] * len(big),
-        out_specs=(hbm, hbm, hbm),
-        scratch_shapes=[pltpu.VMEM(x.shape, x.dtype) for x in big + (fine, coarse)]
+        out_specs=(vm, vm, vm),
+        scratch_shapes=[pltpu.VMEM(x.shape, x.dtype) for x in big]
         + [
             pltpu.VMEM((bands, slots, ins * rows, cols), F32),
             pltpu.VMEM((bands, 3, slab, cols), BF16),
@@ -428,31 +421,26 @@
             pltpu.VMEM((2 * chans, k3), BF16),
             pltpu.VMEM((slots, k1, bands * cols), BF16),
             pltpu.VMEM((slots, k2, bands * cols), BF16),
-            pltpu.VMEM((cr * half, cols), F32),
             pltpu.SemaphoreType.DMA((len(big),)),
             pltpu.SemaphoreType.DMA((2,)),
             pltpu.SemaphoreType.DMA((2,)),
             pltpu.SemaphoreType.DMA((nb * nr - 1,)),
             pltpu.SemaphoreType.DMA((nb * nr - 1,)),
-            pltpu.SemaphoreType.DMA((slots + 2,)),
         ],
         compiler_params=pltpu.CompilerParams(
-            collective_id=0, has_side_effects=True, vmem_limit_bytes=56 * 1024 * 1024
+            collective_id=0, has_side_effects=True, vmem_limit_bytes=24 * 1024 * 1024
         ),
-    )(live, nbrs.T, perm, bu, br, bc, b_coarse, *big)
+    )(*small, *big)
     return pl.pallas_call(
         functools.partial(finish, nb, nr, cs.shape[0]),
         out_shape=(fine, jax.ShapeDtypeStruct(cs.shape, F32)),
-        in_specs=[hbm] * 4,
-        out_specs=(hbm, vm),
+        in_specs=[vm, vm, vm, pl.BlockSpec(memory_space=pl.ANY)],
+        out_specs=(hbm, hbm),
         scratch_shapes=[
-            pltpu.VMEM(pooled.shape, F32),
-            pltpu.VMEM(coarse.shape, F32),
-            pltpu.VMEM(u_pool.shape, F32),
-            pltpu.SemaphoreType.DMA((3,)),
-            pltpu.SemaphoreType.DMA((bands * slots,)),
+            pltpu.VMEM(cs.shape, F32),
+            pltpu.SemaphoreType.DMA((bands * slots + 1,)),
         ],
-        compiler_params=pltpu.CompilerParams(vmem_limit_bytes=56 * 1024 * 1024),
+        compiler_params=pltpu.CompilerParams(vmem_limit_bytes=24 * 1024 * 1024),
     )(parts, held, u_pool, new)
 
 

time: 32.3 us -> 15.5 us (0.48)
  Pallas kernels: 31.4 us -> 14.6 us
    pallas_call x1, Pallas kernels: 17.7 us -> 1.1 us  [shards(): pl.pallas_call(functools.partial(finish, nb, nr, cs.shape[0]), out_shape=...]
where the time goes in v4:
time: 15.5 us; the launch traced here: 15.3 us
  Pallas kernels  14.6 us (94%)
  between operations  0.66 us (4%)
    pallas_call x1, Pallas kernels, shards(): pl.pallas_call(functools.partial(kernel, nt, nb, nr, ins, rows), out_shap...  13.5 us
    pallas_call x1, Pallas kernels, shards(): pl.pallas_call(functools.partial(finish, nb, nr, cs.shape[0]), out_shape=...  1.1 us

profile of v4, /device:TPU:0, one launch (start us, length us, event | category | flops | bytes accessed | tf_op | source)
XLA Modules:
  0.0 15.3 jit_solution(12786564096636736087)
XLA Ops:
  0.6 0.0 copy-start
  0.6 13.5 %shard_map.158 = (f32[2,4,8,16,128]{4,3,2,1,0:T(8,128)S(1)}, f32[4,32,128]{2,1,0:T(8,128)S(1)}, f32[2,16,512]{2,1,0:T(8,128)S(1)}) custom-call(s32[4]{0:T(128)} %live.1, s32[2,4]{1,0:T(2,128)} %bitcast.5, s32[1,4]{1,0:T(1,128)} %perm.1, f32[16]{0:T(128)} %bu.1, f32[16]{0:T(128)} %br.1, f32[16]{0:T(128)} %bc.1, f32[16]{0:T(128)} %b_coarse.1, ...), custom_call_target="tpu_custom_call" | custom-call | tf_op jit(solution)/shard_map/pallas_call | solution.py:398
  14.2 0.0 copy-done
  14.2 1.1 %shard_map.159 = (f32[2,4,8,16,128]{4,3,2,1,0:T(8,128)}, f32[2,16,4,32]{3,2,1,0:T(4,128)}) custom-call(f32[4,32,128]{2,1,0:T(8,128)S(1)} %get-tuple-element.5.parts, f32[2,16,512]{2,1,0:T(8,128)S(1)} %get-tuple-element.6.coarse, f32[16,16]{1,0:T(8,128)S(1)} %copy-done, f32[2,4,8,16,128]{4,3,2,1,0:T(8,128)S(1)} %get-tuple-element.7.new_in), custom_call_target="tpu_custom_call" | custom-call | tf_op jit(solution)/shard_map/pallas_call | solution.py:434
Async XLA Ops:
  0.6 13.6 %copy-start = (f32[16,16]{1,0:T(8,128)S(1)}, f32[16,16]{1,0:T(8,128)}, u32[]{:S(2)}) copy-start(f32[16,16]{1,0:T(8,128)} %u_pool.1) | copy-start | bytes 3076

commit v5 on v4

--- a/solution.py
+++ b/solution.py
@@ -21,6 +21,13 @@
     return 0.5 * jnp.tanh(0.5 * x) + 0.5
 
 
+def thirds(x):
+    high = x.astype(BF16)
+    rest = x - high.astype(F32)
+    middle = rest.astype(BF16)
+    return high, middle, (rest - middle.astype(F32)).astype(BF16)
+
+
 def shifted(x, step):
     width = x.shape[1]
     wide = pltpu.roll(x, (-step) % width, 1)
@@ -30,9 +37,9 @@
 
 def kernel(
     nt, nb, nr, ins, rows,
-    live, nbrs, perm, bu, br, bc, b_coarse, features_in, state_in, cs_in, wu_in, wr_in, wc_in, u_state_in,
+    live_in, nbrs_in, perm_in, bu_in, br_in, bc_in, b_coarse_in, features_in, state_in, cs_in, wu_in, wr_in, wc_in, u_state_in,
     out, parts, coarse,
-    features, state, cs, wu, wr, wc, u_state,
+    live, nbrs, perm, bu, br, bc, b_coarse, features, state, cs, wu, wr, wc, u_state,
     feats, send_up, send_dn, got_up, got_dn, tops, bots, gtops, gbots, strip, gates,
     w1, w2, w3, t1, t2, t3, x1, x2,
     load_sems, up_sems, dn_sems, pool_send, pool_recv,
@@ -58,6 +65,8 @@
             (
                 (wu_in, wu), (wr_in, wr), (wc_in, wc), (features_in, features), (state_in, state),
                 (cs_in, cs), (u_state_in, u_state),
+                (live_in, live), (nbrs_in, nbrs), (perm_in, perm),
+                (bu_in, bu), (br_in, br), (bc_in, bc), (b_coarse_in, b_coarse),
             )
         )
     ]
@@ -80,14 +89,6 @@
         pl.semaphore_signal(
             barrier, inc=1, device_id={"band": peer // nr, "rep": lax.rem(peer, nr)}, device_id_type=MESH
         )
-
-    first = jnp.int32(0)
-    last = jnp.int32(0)
-    for s in range(slots):
-        u, d = nbrs[0, s], nbrs[1, s]
-        alive = live[s] > 0
-        first = jnp.where(alive & ((u < base) | (u >= base + slots)), s, first)
-        last = jnp.where(alive & ((d < base) | (d >= base + slots)), s, last)
 
     def lanes(size, main, halo):
         part = size // 3
@@ -132,6 +133,16 @@
     spread(w1, (wu, wr), km, halo1)
     spread(w2, (wc,), km, halo2)
     spread(w3, (wr,), 0, halo3)
+    for load in loads[7:]:
+        load.wait()
+    first = jnp.int32(0)
+    last = jnp.int32(0)
+    for s in range(slots):
+        u, d = nbrs[0, s], nbrs[1, s]
+        alive = live[s] > 0
+        first = jnp.where(alive & ((u < base) | (u >= base + slots)), s, first)
+        last = jnp.where(alive & ((d < base) | (d >= base + slots)), s, last)
+
     loads[3].wait()
     loads[4].wait()
     for s in range(slots):
@@ -188,7 +199,7 @@
             total = jnp.where(row3 == i - 2 + a - 1, w3[a], total)
         t3[i * chans : (i + 1) * chans] = total.astype(BF16)
 
-    for load in loads[5:]:
+    for load in loads[5:7]:
         load.wait()
     coarse[0] = jnp.zeros_like(coarse[0])
     for k in range(own):
@@ -321,11 +332,13 @@
         gather = jnp.where(
             iota((cols, slots * cw), 1) == spot * cw + (iota((cols, slots * cw), 0) >> 2), 1.0 / 16.0, 0.0
         )
-        pooled = pooled + jnp.dot(summed, gather, precision=HIGHEST, preferred_element_type=F32)
+        product = jnp.dot(jnp.concatenate(thirds(summed), axis=0), gather.astype(BF16), preferred_element_type=F32)
+        pooled = pooled + (product[:mu] + (product[mu : 2 * mu] + product[2 * mu :]))
 
     m, q = iota((cr * half, mu), 0), iota((cr * half, mu), 1)
     rowsum = jnp.where(((m & (half - 1)) == (q >> 4)) & ((m >> (half.bit_length() - 1)) == ((q & (rows - 1)) >> 2)), 1.0, 0.0)
-    parts[me] = jnp.dot(rowsum, pooled, precision=HIGHEST, preferred_element_type=F32)
+    product = jnp.dot(rowsum.astype(BF16), jnp.concatenate(thirds(pooled), axis=1), preferred_element_type=F32)
+    parts[me] = product[:, :cols] + (product[:, cols : 2 * cols] + product[:, 2 * cols :])
 
     copies = []
     for d in range(1, npeer):
@@ -383,7 +396,6 @@
     cr = rows // 4
     hbm = pl.BlockSpec(memory_space=pltpu.HBM)
     vm = pl.BlockSpec(memory_space=pltpu.VMEM)
-    sm = pl.BlockSpec(memory_space=pltpu.SMEM)
     features = features.reshape(bands, slots, ins * rows, cols)
     state = state.reshape(bands, slots, chans * rows, cols)
     big = tuple(
@@ -398,9 +410,10 @@
     new, parts, held = pl.pallas_call(
         functools.partial(kernel, nt, nb, nr, ins, rows),
         out_shape=(fine, pooled, coarse),
-        in_specs=[sm] * 7 + [hbm] * len(big),
+        in_specs=[hbm] * (len(small) + len(big)),
         out_specs=(vm, vm, vm),
-        scratch_shapes=[pltpu.VMEM(x.shape, x.dtype) for x in big]
+        scratch_shapes=[pltpu.SMEM(x.shape, x.dtype) for x in small]
+        + [pltpu.VMEM(x.shape, x.dtype) for x in big]
         + [
             pltpu.VMEM((bands, slots, ins * rows, cols), F32),
             pltpu.VMEM((bands, 3, slab, cols), BF16),
@@ -421,7 +434,7 @@
             pltpu.VMEM((2 * chans, k3), BF16),
             pltpu.VMEM((slots, k1, bands * cols), BF16),
             pltpu.VMEM((slots, k2, bands * cols), BF16),
-            pltpu.SemaphoreType.DMA((len(big),)),
+            pltpu.SemaphoreType.DMA((len(small) + len(big),)),
             pltpu.SemaphoreType.DMA((2,)),
             pltpu.SemaphoreType.DMA((2,)),
             pltpu.SemaphoreType.DMA((nb * nr - 1,)),

time: 15.5 us -> 14.9 us (0.961)
  Pallas kernels: 14.6 us -> 14 us
    pallas_call x1, Pallas kernels: 13.5 us -> 12.9 us  [shards(): pl.pallas_call(functools.partial(kernel, nt, nb, nr, ins, rows), out_shap...]
where the time goes in v5:
time: 14.9 us; the launch traced here: 14.7 us
  Pallas kernels  14 us (94%)
  between operations  0.66 us (4%)
    pallas_call x1, Pallas kernels, shards(): pl.pallas_call(functools.partial(kernel, nt, nb, nr, ins, rows), out_shap...  12.9 us
    pallas_call x1, Pallas kernels, shards(): pl.pallas_call(functools.partial(finish, nb, nr, cs.shape[0]), out_shape=...  1.1 us

profile of v5, /device:TPU:0, one launch (start us, length us, event | category | flops | bytes accessed | tf_op | source)
XLA Modules:
  0.0 14.7 jit_solution(17506943304402685872)
XLA Ops:
  0.6 0.0 copy-start
  0.6 12.9 %shard_map.158 = (f32[2,4,8,16,128]{4,3,2,1,0:T(8,128)S(1)}, f32[4,32,128]{2,1,0:T(8,128)S(1)}, f32[2,16,512]{2,1,0:T(8,128)S(1)}) custom-call(s32[4]{0:T(128)} %live_in.1, s32[2,4]{1,0:T(2,128)} %bitcast.5, s32[1,4]{1,0:T(1,128)} %perm_in.1, f32[16]{0:T(128)} %bu_in.1, f32[16]{0:T(128)} %br_in.1, f32[16]{0:T(128)} %bc_in.1, f32[16]{0:T(128)} %b_coarse_in.1, ...), custom_call_target="tpu_custom_call" | custom-call | tf_op jit(solution)/shard_map/pallas_call | solution.py:410
  13.6 0.0 copy-done
  13.6 1.1 %shard_map.159 = (f32[2,4,8,16,128]{4,3,2,1,0:T(8,128)}, f32[2,16,4,32]{3,2,1,0:T(4,128)}) custom-call(f32[4,32,128]{2,1,0:T(8,128)S(1)} %get-tuple-element.5.parts, f32[2,16,512]{2,1,0:T(8,128)S(1)} %get-tuple-element.6.coarse, f32[16,16]{1,0:T(8,128)S(1)} %copy-done, f32[2,4,8,16,128]{4,3,2,1,0:T(8,128)S(1)} %get-tuple-element.7.new_in), custom_call_target="tpu_custom_call" | custom-call | tf_op jit(solution)/shard_map/pallas_call | solution.py:447
Async XLA Ops:
  0.6 13.0 %copy-start = (f32[16,16]{1,0:T(8,128)S(1)}, f32[16,16]{1,0:T(8,128)}, u32[]{:S(2)}) copy-start(f32[16,16]{1,0:T(8,128)} %u_pool.1) | copy-start | bytes 3076

commit v6 on v5

--- a/solution.py
+++ b/solution.py
@@ -30,9 +30,10 @@
 
 def shifted(x, step):
     width = x.shape[1]
-    wide = pltpu.roll(x, (-step) % width, 1)
-    column = iota(x.shape, 1) + step
-    return jnp.where((column >= 0) & (column < width), wide, jnp.zeros_like(wide))
+    wide = pltpu.roll(x, (-step) % width, 1).reshape(-1, 16, width)
+    column = iota((16, width), 1) + step
+    keep = ((column >= 0) & (column < width)).astype(F32).astype(BF16)
+    return (wide * keep[None]).reshape(x.shape)
 
 
 def kernel(
@@ -63,14 +64,19 @@
         pltpu.make_async_copy(src, dst, load_sems.at[i])
         for i, (src, dst) in enumerate(
             (
-                (wu_in, wu), (wr_in, wr), (wc_in, wc), (features_in, features), (state_in, state),
+                (wu_in, wu), (wr_in, wr), (wc_in, wc), (features_in, features),
                 (cs_in, cs), (u_state_in, u_state),
                 (live_in, live), (nbrs_in, nbrs), (perm_in, perm),
                 (bu_in, bu), (br_in, br), (bc_in, bc), (b_coarse_in, b_coarse),
             )
         )
     ]
-    for load in loads:
+    state_loads = [
+        pltpu.make_async_copy(state_in.at[b, s], state.at[b, s], load_sems.at[len(loads) + b * slots + s])
+        for b in range(bands)
+        for s in range(slots)
+    ]
+    for load in loads[:4] + state_loads + loads[4:]:
         load.start()
 
     barrier = pltpu.get_barrier_semaphore()
@@ -133,7 +139,7 @@
     spread(w1, (wu, wr), km, halo1)
     spread(w2, (wc,), km, halo2)
     spread(w3, (wr,), 0, halo3)
-    for load in loads[7:]:
+    for load in loads[6:]:
         load.wait()
     first = jnp.int32(0)
     last = jnp.int32(0)
@@ -143,8 +149,8 @@
         first = jnp.where(alive & ((u < base) | (u >= base + slots)), s, first)
         last = jnp.where(alive & ((d < base) | (d >= base + slots)), s, last)
 
-    loads[3].wait()
-    loads[4].wait()
+    for load in loads[3:4] + state_loads:
+        load.wait()
     for s in range(slots):
         for b in range(bands):
             feats[b, s] = features[b, s].astype(F32)
@@ -199,7 +205,7 @@
             total = jnp.where(row3 == i - 2 + a - 1, w3[a], total)
         t3[i * chans : (i + 1) * chans] = total.astype(BF16)
 
-    for load in loads[5:7]:
+    for load in loads[4:6]:
         load.wait()
     coarse[0] = jnp.zeros_like(coarse[0])
     for k in range(own):
@@ -434,7 +440,7 @@
             pltpu.VMEM((2 * chans, k3), BF16),
             pltpu.VMEM((slots, k1, bands * cols), BF16),
             pltpu.VMEM((slots, k2, bands * cols), BF16),
-            pltpu.SemaphoreType.DMA((len(small) + len(big),)),
+            pltpu.SemaphoreType.DMA((len(small) + len(big) + bands * slots,)),
             pltpu.SemaphoreType.DMA((2,)),
             pltpu.SemaphoreType.DMA((2,)),
             pltpu.SemaphoreType.DMA((nb * nr - 1,)),

time: 14.9 us -> 14.9 us (level)
  no operation moved by 1% of the time
where the time goes in v6:
time: 14.9 us; the launch traced here: 14.8 us
  Pallas kernels  14.1 us (95%)
  between operations  0.66 us (4%)
    pallas_call x1, Pallas kernels, shards(): pl.pallas_call(functools.partial(kernel, nt, nb, nr, ins, rows), out_shap...  13 us
    pallas_call x1, Pallas kernels, shards(): pl.pallas_call(functools.partial(finish, nb, nr, cs.shape[0]), out_shape=...  1.1 us

profile of v6, /device:TPU:0, one launch (start us, length us, event | category | flops | bytes accessed | tf_op | source)
XLA Modules:
  0.0 14.8 jit_solution(4934264283349332549)
XLA Ops:
  0.6 0.0 copy-start
  0.6 13.0 %shard_map.158 = (f32[2,4,8,16,128]{4,3,2,1,0:T(8,128)S(1)}, f32[4,32,128]{2,1,0:T(8,128)S(1)}, f32[2,16,512]{2,1,0:T(8,128)S(1)}) custom-call(s32[4]{0:T(128)} %live_in.1, s32[2,4]{1,0:T(2,128)} %bitcast.5, s32[1,4]{1,0:T(1,128)} %perm_in.1, f32[16]{0:T(128)} %bu_in.1, f32[16]{0:T(128)} %br_in.1, f32[16]{0:T(128)} %bc_in.1, f32[16]{0:T(128)} %b_coarse_in.1, ...), custom_call_target="tpu_custom_call" | custom-call | tf_op jit(solution)/shard_map/pallas_call | solution.py:416
  13.7 0.0 copy-done
  13.7 1.1 %shard_map.159 = (f32[2,4,8,16,128]{4,3,2,1,0:T(8,128)}, f32[2,16,4,32]{3,2,1,0:T(4,128)}) custom-call(f32[4,32,128]{2,1,0:T(8,128)S(1)} %get-tuple-element.5.parts, f32[2,16,512]{2,1,0:T(8,128)S(1)} %get-tuple-element.6.coarse, f32[16,16]{1,0:T(8,128)S(1)} %copy-done, f32[2,4,8,16,128]{4,3,2,1,0:T(8,128)S(1)} %get-tuple-element.7.new_in), custom_call_target="tpu_custom_call" | custom-call | tf_op jit(solution)/shard_map/pallas_call | solution.py:453
Async XLA Ops:
  0.6 13.0 %copy-start = (f32[16,16]{1,0:T(8,128)S(1)}, f32[16,16]{1,0:T(8,128)}, u32[]{:S(2)}) copy-start(f32[16,16]{1,0:T(8,128)} %u_pool.1) | copy-start | bytes 3076

commit v7 on v6

--- a/solution.py
+++ b/solution.py
@@ -125,12 +125,16 @@
         delta = row - iota(shape, 0)
         hits = [(delta == a * dilation).astype(F32).astype(BF16) for a in (-1, 0, 1)]
         for at, gate, outs, count in jobs:
-            for o in range(count):
+
+            def step(o, carry, at=at, gate=gate, outs=outs):
                 total = None
                 for a in range(3):
                     line = jnp.broadcast_to(source[3 * gate + a, pl.ds(outs + o, 1), :], shape).astype(BF16)
                     total = line * hits[a] if total is None else total + line * hits[a]
-                target[at + o * rows : at + (o + 1) * rows, :] = total
+                target[pl.ds(pl.multiple_of(at + o * rows, rows), rows), :] = total
+                return carry
+
+            lax.fori_loop(0, count, step, 0, unroll=2)
 
     mu = half * rows
     halo1, halo2, halo3 = (-1, rows), (-2, -1, rows, rows + 1), (-3, -2, -1, 0)
@@ -217,7 +221,7 @@
     coarse[1] = jnp.dot(u_state[...], coarse[0], precision=HIGHEST, preferred_element_type=F32) + coarse_bias
 
     k1, k2 = km + 2 * slab, km + 4 * slab
-    for s in range(slots):
+    def prepare(s, carry):
         for b in range(bands):
             at = slice(b * cols, (b + 1) * cols)
             tops[s, b] = row_slab(b, s, 0)
@@ -228,6 +232,10 @@
                 x1[s, j * k1 : j * k1 + flat, at] = shifted(x, step) if step else x
                 x1[s, j * k1 + flat : j * k1 + km, at] = shifted(f, step) if step else f
                 x2[s, j * k2 + flat : j * k2 + km, at] = shifted(f, 2 * step) if step else f
+        return carry
+
+    lax.fori_loop(0, slots, prepare, 0)
+
     tops[slots + 1] = jnp.zeros((bands, slab, cols), BF16)
     bots[slots + 1] = jnp.zeros((bands, slab, cols), BF16)
     gtops[slots + 1] = jnp.zeros((bands, 2, slab, cols), BF16)
@@ -260,8 +268,7 @@
         here = (n >= base) & (n < base + slots)
         return jnp.where(here, n - base, jnp.where(n >= 0, slots, slots + 1))
 
-    updates = []
-    for s in range(slots):
+    def gate(s, carry):
         above, below = place(s, 0), place(s, 1)
         for b in range(bands):
             at = slice(b * cols, (b + 1) * cols)
@@ -284,6 +291,9 @@
                 for target, row in ((gtops, i), (gbots, rows - 2 + i)):
                     g = gates[s, b, pl.ds(mu + row, chans, stride=rows), :]
                     target[s, b, i] = jnp.concatenate([g, feat_rows(b, s, row)], axis=0).astype(BF16)
+        return carry
+
+    lax.fori_loop(0, slots, gate, 0)
 
     for b in range(bands):
         for side in range(2):
@@ -309,8 +319,7 @@
                 else:
                     gtops[slots, b, i] = joined
 
-    pooled = jnp.zeros((mu, slots * cw), F32)
-    for s in range(slots):
+    def renew(s, pooled):
         above, below = place(s, 0), place(s, 1)
         for b in range(bands):
             at = slice(b * cols, (b + 1) * cols)
@@ -340,6 +349,9 @@
         )
         product = jnp.dot(jnp.concatenate(thirds(summed), axis=0), gather.astype(BF16), preferred_element_type=F32)
         pooled = pooled + (product[:mu] + (product[mu : 2 * mu] + product[2 * mu :]))
+        return pooled
+
+    pooled = lax.fori_loop(0, slots, renew, jnp.zeros((mu, slots * cw), F32))
 
     m, q = iota((cr * half, mu), 0), iota((cr * half, mu), 1)
     rowsum = jnp.where(((m & (half - 1)) == (q >> 4)) & ((m >> (half.bit_length() - 1)) == ((q & (rows - 1)) >> 2)), 1.0, 0.0)

time: 14.9 us -> 17 us (1.14)
  Pallas kernels: 14.1 us -> 16.2 us
    pallas_call x1, Pallas kernels: 13 us -> 15 us  [shards(): pl.pallas_call(functools.partial(kernel, nt, nb, nr, ins, rows), out_shap...]
where the time goes in v7:
time: 17 us; the launch traced here: 16.8 us
  Pallas kernels  16.2 us (95%)
  between operations  0.66 us (4%)
    pallas_call x1, Pallas kernels, shards(): pl.pallas_call(functools.partial(kernel, nt, nb, nr, ins, rows), out_shap...  15 us
    pallas_call x1, Pallas kernels, shards(): pl.pallas_call(functools.partial(finish, nb, nr, cs.shape[0]), out_shape=...  1.1 us

profile of v7, /device:TPU:0, one launch (start us, length us, event | category | flops | bytes accessed | tf_op | source)
XLA Modules:
  0.0 16.8 jit_solution(6860234679429787829)
XLA Ops:
  0.6 0.0 copy-start
  0.6 15.0 %shard_map.158 = (f32[2,4,8,16,128]{4,3,2,1,0:T(8,128)S(1)}, f32[4,32,128]{2,1,0:T(8,128)S(1)}, f32[2,16,512]{2,1,0:T(8,128)S(1)}) custom-call(s32[4]{0:T(128)} %live_in.1, s32[2,4]{1,0:T(2,128)} %bitcast.5, s32[1,4]{1,0:T(1,128)} %perm_in.1, f32[16]{0:T(128)} %bu_in.1, f32[16]{0:T(128)} %br_in.1, f32[16]{0:T(128)} %bc_in.1, f32[16]{0:T(128)} %b_coarse_in.1, ...), custom_call_target="tpu_custom_call" | custom-call | tf_op jit(solution)/shard_map/pallas_call | solution.py:428
  15.7 0.0 copy-done
  15.7 1.1 %shard_map.159 = (f32[2,4,8,16,128]{4,3,2,1,0:T(8,128)}, f32[2,16,4,32]{3,2,1,0:T(4,128)}) custom-call(f32[4,32,128]{2,1,0:T(8,128)S(1)} %get-tuple-element.5.parts, f32[2,16,512]{2,1,0:T(8,128)S(1)} %get-tuple-element.6.coarse, f32[16,16]{1,0:T(8,128)S(1)} %copy-done, f32[2,4,8,16,128]{4,3,2,1,0:T(8,128)S(1)} %get-tuple-element.7.new_in), custom_call_target="tpu_custom_call" | custom-call | tf_op jit(solution)/shard_map/pallas_call | solution.py:465
Async XLA Ops:
  0.6 15.1 %copy-start = (f32[16,16]{1,0:T(8,128)S(1)}, f32[16,16]{1,0:T(8,128)}, u32[]{:S(2)}) copy-start(f32[16,16]{1,0:T(8,128)} %u_pool.1) | copy-start | bytes 3076

commit v8 on v6

--- a/solution.py
+++ b/solution.py
@@ -42,7 +42,7 @@
     out, parts, coarse,
     live, nbrs, perm, bu, br, bc, b_coarse, features, state, cs, wu, wr, wc, u_state,
     feats, send_up, send_dn, got_up, got_dn, tops, bots, gtops, gbots, strip, gates,
-    w1, w2, w3, t1, t2, t3, x1, x2,
+    w1, wh, w2, w3, t1, th, t2, t3, x1, xh, x2, sums,
     load_sems, up_sems, dn_sems, pool_send, pool_recv,
 ):
     bands, slots, flat, cols = state.shape
@@ -136,7 +136,8 @@
     halo1, halo2, halo3 = (-1, rows), (-2, -1, rows, rows + 1), (-3, -2, -1, 0)
     for load in loads[:3]:
         load.wait()
-    spread(w1, (wu, wr), km, halo1)
+    spread(w1, (wu, wr), km, ())
+    spread(wh, (wu, wr), 0, halo1)
     spread(w2, (wc,), km, halo2)
     spread(w3, (wr,), 0, halo3)
     for load in loads[6:]:
@@ -196,7 +197,8 @@
     def _():
         got_dn[...] = jnp.zeros_like(got_dn)
 
-    fill(t1, w1, ((0, 0, start, half), (mu, 1, 0, chans)), km, halo1, 1)
+    fill(t1, w1, ((0, 0, start, half), (mu, 1, 0, chans)), km, (), 1)
+    fill(th, wh, ((0, 0, start, half), (mu, 1, 0, chans)), 0, halo1, 1)
     fill(t2, w2, ((0, 0, start, half),), km, halo2, 2)
     _, row3 = lanes(t3.shape[1], 0, halo3)
     for i in range(2):
@@ -216,7 +218,7 @@
         coarse_bias = jnp.where(iota((chans, 1), 0) == o, b_coarse[o], coarse_bias)
     coarse[1] = jnp.dot(u_state[...], coarse[0], precision=HIGHEST, preferred_element_type=F32) + coarse_bias
 
-    k1, k2 = km + 2 * slab, km + 4 * slab
+    k1, kh, k2 = km, 2 * slab, km + 4 * slab
     for s in range(slots):
         for b in range(bands):
             at = slice(b * cols, (b + 1) * cols)
@@ -228,6 +230,7 @@
                 x1[s, j * k1 : j * k1 + flat, at] = shifted(x, step) if step else x
                 x1[s, j * k1 + flat : j * k1 + km, at] = shifted(f, step) if step else f
                 x2[s, j * k2 + flat : j * k2 + km, at] = shifted(f, 2 * step) if step else f
+        sums[s] = jnp.dot(t1[...], x1[s], preferred_element_type=F32)
     tops[slots + 1] = jnp.zeros((bands, slab, cols), BF16)
     bots[slots + 1] = jnp.zeros((bands, slab, cols), BF16)
     gtops[slots + 1] = jnp.zeros((bands, 2, slab, cols), BF16)
@@ -267,8 +270,8 @@
             at = slice(b * cols, (b + 1) * cols)
             x = jnp.concatenate([bots[above, b], tops[below, b]], axis=0)
             for j, step in enumerate((-1, 0, 1)):
-                x1[s, j * k1 + km : (j + 1) * k1, at] = shifted(x, step) if step else x
-        acc = jnp.dot(t1[...], x1[s], preferred_element_type=F32)
+                xh[s, j * kh : (j + 1) * kh, at] = shifted(x, step) if step else x
+        acc = sums[s] + jnp.dot(th[...], xh[s], preferred_element_type=F32)
         for b in range(bands):
             at = slice(b * cols, (b + 1) * cols)
             for o in range(half):
@@ -398,7 +401,7 @@
     half = chans // nr
     km = width * rows
     slab = 32
-    k1, k2, k3 = 3 * (km + 2 * slab), 3 * (km + 4 * slab), 12 * slab
+    k1, kh, k2, k3 = 3 * km, 6 * slab, 3 * (km + 4 * slab), 12 * slab
     cr = rows // 4
     hbm = pl.BlockSpec(memory_space=pltpu.HBM)
     vm = pl.BlockSpec(memory_space=pltpu.VMEM)
@@ -433,13 +436,17 @@
             pltpu.VMEM((k3, 2 * bands * cols), BF16),
             pltpu.VMEM((slots, bands, (half + chans) * rows, cols), F32),
             pltpu.VMEM((6, chans, k1), F32),
+            pltpu.VMEM((6, chans, kh), F32),
             pltpu.VMEM((3, chans, k2), F32),
             pltpu.VMEM((3, chans, k3), F32),
             pltpu.VMEM(((half + chans) * rows, k1), BF16),
+            pltpu.VMEM(((half + chans) * rows, kh), BF16),
             pltpu.VMEM((half * rows, k2), BF16),
             pltpu.VMEM((2 * chans, k3), BF16),
             pltpu.VMEM((slots, k1, bands * cols), BF16),
+            pltpu.VMEM((slots, kh, bands * cols), BF16),
             pltpu.VMEM((slots, k2, bands * cols), BF16),
+            pltpu.VMEM((slots, (half + chans) * rows, bands * cols), F32),
             pltpu.SemaphoreType.DMA((len(small) + len(big) + bands * slots,)),
             pltpu.SemaphoreType.DMA((2,)),
             pltpu.SemaphoreType.DMA((2,)),

time: 14.9 us -> 14.4 us (0.966)
  Pallas kernels: 14.1 us -> 13.6 us
    pallas_call x1, Pallas kernels: 13 us -> 12.5 us  [shards(): pl.pallas_call(functools.partial(kernel, nt, nb, nr, ins, rows), out_shap...]
where the time goes in v8:
time: 14.4 us; the launch traced here: 14.3 us
  Pallas kernels  13.6 us (94%)
  between operations  0.66 us (5%)
    pallas_call x1, Pallas kernels, shards(): pl.pallas_call(functools.partial(kernel, nt, nb, nr, ins, rows), out_shap...  12.5 us
    pallas_call x1, Pallas kernels, shards(): pl.pallas_call(functools.partial(finish, nb, nr, cs.shape[0]), out_shape=...  1.1 us

profile of v8, /device:TPU:0, one launch (start us, length us, event | category | flops | bytes accessed | tf_op | source)
XLA Modules:
  0.0 14.3 jit_solution(17488359337614720189)
XLA Ops:
  0.6 0.0 copy-start
  0.6 12.5 %shard_map.158 = (f32[2,4,8,16,128]{4,3,2,1,0:T(8,128)S(1)}, f32[4,32,128]{2,1,0:T(8,128)S(1)}, f32[2,16,512]{2,1,0:T(8,128)S(1)}) custom-call(s32[4]{0:T(128)} %live_in.1, s32[2,4]{1,0:T(2,128)} %bitcast.5, s32[1,4]{1,0:T(1,128)} %perm_in.1, f32[16]{0:T(128)} %bu_in.1, f32[16]{0:T(128)} %br_in.1, f32[16]{0:T(128)} %bc_in.1, f32[16]{0:T(128)} %b_coarse_in.1, ...), custom_call_target="tpu_custom_call" | custom-call | tf_op jit(solution)/shard_map/pallas_call | solution.py:419
  13.2 0.0 copy-done
  13.2 1.1 %shard_map.159 = (f32[2,4,8,16,128]{4,3,2,1,0:T(8,128)}, f32[2,16,4,32]{3,2,1,0:T(4,128)}) custom-call(f32[4,32,128]{2,1,0:T(8,128)S(1)} %get-tuple-element.5.parts, f32[2,16,512]{2,1,0:T(8,128)S(1)} %get-tuple-element.6.coarse, f32[16,16]{1,0:T(8,128)S(1)} %copy-done, f32[2,4,8,16,128]{4,3,2,1,0:T(8,128)S(1)} %get-tuple-element.7.new_in), custom_call_target="tpu_custom_call" | custom-call | tf_op jit(solution)/shard_map/pallas_call | solution.py:460
Async XLA Ops:
  0.6 12.5 %copy-start = (f32[16,16]{1,0:T(8,128)S(1)}, f32[16,16]{1,0:T(8,128)}, u32[]{:S(2)}) copy-start(f32[16,16]{1,0:T(8,128)} %u_pool.1) | copy-start | bytes 3076
